TPU v7x, 512 devices: a whole 4x4x16 slice. The times are simulated.
512 devices in a mesh: section: 8 (over y, x_lo), tp: 64 (over z, x_hi, core).
Axes of the slice: x: 4 (x_hi: 2, x_lo: 2; x = x_hi * 2 + x_lo), y: 4, z: 16, core: 2. Of those that a mesh axis runs over, the one named last changes fastest.
Arguments:
- hidden_in: bfloat16 [8, 8, 4096], P('section', None, 'tp'), may hold values from -6 to 6
- norm_gain: float32 [8, 4096], P('section'), may hold values from 0.25 to 1.75
- w_qkv: bfloat16 [8, 4096, 6144], P('section', None, 'tp'), may hold values from -0.09375 to 0.09375
- w_out: bfloat16 [8, 4096, 4096], P('section', None, 'tp'), may hold values from -0.09375 to 0.09375
- paged_key_codes: bfloat16 [8, 512, 64, 1024], P('section', 'tp'), may hold values from -127 to 127, as said below
- paged_value_codes: bfloat16 [8, 512, 64, 1024], P('section', 'tp'), may hold values from -127 to 127, as said below
- paged_scale_table: float32 [8, 512, 2, 8], P('section', 'tp'), may hold values from 0.005 to 1
- page_owner: int32 [8, 512], P('section', 'tp'), may hold values from 0 to 16, as said below
- page_pos: int32 [8, 512], P('section', 'tp'), may hold values from 0 to 127, as said below
- lengths: int32 [8, 16], P('section'), may hold values from 1 to 8192, as said below
- row_assign: int32 [8, 8], P('section'), may hold values from 0 to 15, as said below
Outputs:
- hidden_out: float32 [8, 8, 4096], P('section', None, 'tp')
Inputs may be any that keep to these rules, and one draw needn't show every extreme that they name: `paged_key_codes`: whole numbers. `paged_value_codes`: whole numbers. `page_owner`: A slot holding 16 is free; every section has a free slot, and every request holds at least one page. `page_pos`: the slots of one request carry its page numbers 0, 1, ... up to its page count minus one, each once; a free slot carries 0. One request of every section holds 128 pages. `lengths`: A request holding n pages has a length from (n - 1) * 64 + 1 to n * 64; the request holding 128 pages has length 8192. `row_assign`: the rows of one section name distinct requests, request 16 - 1 among them.
All inputs are finite; a program needn't handle non-finite values.
Results may differ from a plain program's by a relative error of at most 0.014.
The roundings to bfloat16 on the way count: a program that leaves them out, or rounds other values in their place, can miss the bound.
Values may be sent and summed in bfloat16 or wider, within the bound.
A program may use at most 64 MiB of HBM per device.

v0:
```python
import jax
import jax.numpy as jnp
from jax import lax
from jax.sharding import PartitionSpec as P

QUERY_HEADS = 32
KEY_VALUE_HEADS = 8
HEAD_SIZE = 128
PAGE_TOKENS = 64
QUERY_WIDTH = 4096
KEY_TOKEN_WIDTH = 1024


rope_base = 500000.0


def passed_along(block, axis, distance):
    devices = range(lax.axis_size(axis))
    route = [((i - distance) % len(devices), i) for i in devices]
    return lax.ppermute(block, axis, route)


def combined_all(array, axis, combine):
    everything = jax.tree.map(lambda part: lax.all_gather(part, axis), array)
    leading = jax.tree.map(lambda part: part[0], everything)

    def hop(k, so_far):
        return combine(so_far, jax.tree.map(lambda part: part[k], everything))

    return lax.fori_loop(1, lax.axis_size(axis), hop, leading)


def apply_rotation(heads, token_position):
    half = heads.shape[-1] // 2
    freq = rope_base ** (-jnp.arange(half, dtype=jnp.float32) / half)
    angle = token_position.astype(jnp.float32)[:, None, None] * freq[None, None, :]
    cosine = jnp.cos(angle)
    sine = jnp.sin(angle)
    first = heads[..., :half]
    second = heads[..., half:]
    return jnp.concatenate(
        [first * cosine - second * sine, second * cosine + first * sine], axis=-1
    )


def restore_codes(stored_codes, scales):
    reshaped_rows = stored_codes.astype(jnp.float32).reshape(
        stored_codes.shape[0], PAGE_TOKENS, KEY_VALUE_HEADS, HEAD_SIZE
    )
    return (
        (reshaped_rows * scales[:, None, :, None])
        .astype(jnp.bfloat16)
        .reshape(stored_codes.shape[0] * PAGE_TOKENS, KEY_TOKEN_WIDTH)
    )


def lookup(table, wanted):
    count = table.shape[0]
    hits = wanted[:, None] == jnp.arange(count, dtype=jnp.int32)[None, :]
    return jnp.sum(jnp.where(hits, table[None, :], 0), axis=1)


def combine(left, right):
    top = jnp.maximum(left[0], right[0])
    scale_left = jnp.exp(left[0] - top)
    scale_right = jnp.exp(right[0] - top)
    return (
        top,
        left[1] * scale_left + right[1] * scale_right,
        left[2] * scale_left[..., None] + right[2] * scale_right[..., None],
    )


def token_mask(owner, numbers, lengths_here, rows_here):
    tok_owner = jnp.repeat(owner, PAGE_TOKENS)
    tok_pos = (
        numbers[:, None] * PAGE_TOKENS + jnp.arange(PAGE_TOKENS, dtype=jnp.int32)[None, :]
    ).reshape(-1)
    limit = lookup(lengths_here, rows_here)
    return (tok_owner[None, :] == rows_here[:, None]) & (tok_pos[None, :] < limit[:, None])


def masked_scores(query_rows, key_rows, mask):
    request_count = query_rows.shape[0]
    query_group = QUERY_HEADS // KEY_VALUE_HEADS
    heads_of_queries = query_rows.reshape(request_count, KEY_VALUE_HEADS, query_group, HEAD_SIZE)
    heads_of_keys = key_rows.reshape(-1, KEY_VALUE_HEADS, HEAD_SIZE)
    scores = jnp.einsum(
        "rgqd,tgd->rgqt", heads_of_queries, heads_of_keys, preferred_element_type=jnp.float32
    ) * (1.0 / HEAD_SIZE**0.5)
    return jnp.where(mask[:, None, None, :], scores, -1e30)


def weigh(masked, mask, peak, value_matrix):
    weights = jnp.where(mask[:, None, None, :], jnp.exp(masked - peak[..., None]), 0.0)
    total = jnp.sum(weights, axis=-1)
    heads_of_values = value_matrix.reshape(-1, KEY_VALUE_HEADS, HEAD_SIZE)
    weighted = jnp.einsum(
        "rgqt,tgd->rgqd",
        weights.astype(jnp.bfloat16),
        heads_of_values,
        preferred_element_type=jnp.float32,
    )
    return (total, weighted)


def partial_softmax(query_rows, key_rows, value_matrix, mask):
    masked = masked_scores(query_rows, key_rows, mask)
    top = jnp.max(masked, axis=-1)
    total, weighted = weigh(masked, mask, top, value_matrix)
    return (top, total, weighted)


def local(
    hidden_in,
    norm_gain,
    w_qkv,
    w_out,
    paged_key_codes,
    paged_value_codes,
    paged_scale_table,
    page_owner,
    page_pos,
    lengths,
    row_assign,
):
    query_group = QUERY_HEADS // KEY_VALUE_HEADS
    inverse_square_root = 1.0 / HEAD_SIZE**0.5
    keys_here = restore_codes(paged_key_codes[0], paged_scale_table[0][:, 0])
    values_here = restore_codes(paged_value_codes[0], paged_scale_table[0][:, 1])
    x_shard, lengths_seen, rows_seen = passed_along((hidden_in, lengths, row_assign), "section", 1)
    x_local = x_shard[0]
    x_full = lax.all_gather(x_local, "tp", axis=1, tiled=True)
    request_count = x_full.shape[0]
    widened = x_full.astype(jnp.float32)
    normed = (
        widened
        * lax.rsqrt(jnp.mean(widened * widened, axis=-1, keepdims=True) + 1e-05)
        * norm_gain[0][None, :]
    ).astype(jnp.bfloat16)
    qkv_local = jnp.dot(normed, w_qkv[0], preferred_element_type=jnp.float32).astype(jnp.bfloat16)
    token_position = lookup(lengths_seen[0], rows_seen[0])
    query_key_value = lax.all_gather(qkv_local, "tp", axis=1, tiled=True)
    query_rows = (
        apply_rotation(
            query_key_value[:, :QUERY_WIDTH]
            .astype(jnp.float32)
            .reshape(request_count, QUERY_HEADS, HEAD_SIZE),
            token_position,
        )
        .astype(jnp.bfloat16)
        .reshape(request_count, QUERY_WIDTH)
    )
    fresh_key = apply_rotation(
        query_key_value[:, QUERY_WIDTH : QUERY_WIDTH + KEY_TOKEN_WIDTH]
        .astype(jnp.float32)
        .reshape(request_count, KEY_VALUE_HEADS, HEAD_SIZE),
        token_position,
    ).astype(jnp.bfloat16)
    fresh_value = (
        query_key_value[:, QUERY_WIDTH + KEY_TOKEN_WIDTH :]
        .reshape(request_count, KEY_VALUE_HEADS, 1, HEAD_SIZE)
        .astype(jnp.float32)
    )
    heads_of_queries = query_rows.astype(jnp.float32).reshape(
        request_count, KEY_VALUE_HEADS, query_group, HEAD_SIZE
    )
    owned_pages = (
        jnp.sum(
            heads_of_queries
            * fresh_key.astype(jnp.float32).reshape(request_count, KEY_VALUE_HEADS, 1, HEAD_SIZE),
            axis=-1,
        )
        * inverse_square_root
    )
    query_back = passed_along(query_rows, "section", -1)
    mask = token_mask(page_owner[0], page_pos[0], lengths[0], row_assign[0])
    top_part, total_part, weighted_part = partial_softmax(query_back, keys_here, values_here, mask)
    top_held, total_held, weighted_held = combined_all(
        (top_part, total_part, weighted_part), "tp", combine
    )
    top, total, weighted = passed_along((top_held, total_held, weighted_held), "section", 1)
    peak = jnp.maximum(top, owned_pages)
    old_weight = jnp.exp(top - peak)
    own_weight = jnp.exp(owned_pages - peak)
    attended = (
        (
            (weighted * old_weight[..., None] + own_weight[..., None] * fresh_value)
            / (total * old_weight + own_weight)[..., None]
        )
        .astype(jnp.bfloat16)
        .reshape(request_count, QUERY_WIDTH)
    )
    output = jnp.dot(attended, w_out[0], preferred_element_type=jnp.float32) + x_local.astype(
        jnp.float32
    )
    return output[None]


def solution(mesh):
    in_specs = (
        P("section", None, "tp"),
        P("section", None),
        P("section", None, "tp"),
        P("section", None, "tp"),
        P("section", "tp", None, None),
        P("section", "tp", None, None),
        P("section", "tp", None, None),
        P("section", "tp"),
        P("section", "tp"),
        P("section", None),
        P("section", None),
    )
    out_specs = P("section", None, "tp")
    return jax.shard_map(local, mesh=mesh, in_specs=in_specs, out_specs=out_specs, check_vma=False)
```

profile of v0, /device:TPU:1, one launch (start us, length us, event | category | flops | bytes accessed | tf_op | source)
XLA Modules:
  0.0 496.6 jit_solution(6770740046808193861)
XLA Ops:
  6.5 4.1 collective-permute-start.2
  10.6 3.2 collective-permute-start.1
  13.8 3.1 collective-permute-start
  20.6 91.1 %all-gather = bf16[1,8,4096]{1,0,2:T(2,128)(2,1)S(1)} all-gather(bf16[1,8,64]{1,0,2:T(2,128)(2,1)S(1)} %copy.83), channel_id=2, replica_groups=mesh['section'=8,'tp'=64] {'tp'}, dimensions={2}, use_global_device_ids=true | all-gather | bytes 66560 | tf_op jit(solution)/shard_map/all_gather | solution.py:133
  111.7 2.2 convert_element_type.110
  114.6 1.3 fusion.8
  115.9 71.9 %all-gather.4 = bf16[64,96,8]{1,2,0:T(8,128)(2,1)S(1)} all-gather(bf16[1,96,8]{1,2,0:T(8,128)(2,1)S(1)} %fusion.8), channel_id=1, replica_groups=mesh['section'=8,'tp'=64] {'tp'}, dimensions={0}, use_global_device_ids=true | all-gather | bytes 99840 | tf_op jit(solution)/shard_map/all_gather | solution.py:143
  188.3 2.9 collective-permute-start.3
  192.3 1.6 collective-permute-done.3
  193.9 1.1 fusion.37
  195.0 1.6 convolution_bitcast_fusion
  197.2 78.4 %all-gather.1 = f32[512,8,4]{1,2,0:T(4,128)S(1)} all-gather(f32[8,8,4]{1,2,0:T(4,128)S(1)} %copy.85), channel_id=3, replica_groups=mesh['section'=8,'tp'=64] {'tp'}, dimensions={0}, use_global_device_ids=true | all-gather | bytes 66560 | tf_op jit(solution)/shard_map/all_gather | solution.py:24
  275.7 75.0 %all-gather.2 = f32[512,8,4]{1,2,0:T(4,128)S(1)} all-gather(f32[8,8,4]{1,2,0:T(4,128)S(1)} %copy.86), channel_id=4, replica_groups=mesh['section'=8,'tp'=64] {'tp'}, dimensions={0}, use_global_device_ids=true | all-gather | bytes 66560 | tf_op jit(solution)/shard_map/all_gather | solution.py:24
  350.7 18.3 %all-gather.7.cloned.1.call-done = f32[512,8,4,128]{3,0,2,1:T(8,128)} async-done(((f32[8,8,4,128]{3,0,2,1:T(8,128)}), f32[512,8,4,128]{3,0,2,1:T(8,128)}) %all-gather.7.cloned.1.call-update) | async-done | bytes 8388624 | tf_op jit(solution)/shard_map/all_gather | solution.py:24
  369.9 103.3 %while.19 = (s32[]{:T(128)}, f32[8,8,4]{1,2,0:T(4,128)S(1)}, f32[8,8,4]{1,2,0:T(4,128)S(1)}, f32[8,8,4,128]{3,2,1,0:T(4,128)S(1)}, f32[64,8,8,4]{2,3,1,0:T(4,128...) while((s32[]{:T(128)}, f32[8,8,4]{1,2,0:T(4,128)S(1)}, ...), condition=%wide.region_6.7_spmd, body=%wide.region_5.6_spmd.sunk | while | flops 99845 | bytes 669839 | solution.py:30
  370.2 0.9 constant_dynamic-slice_fusion.2
  371.9 0.9 constant_dynamic-slice_fusion.2
  373.5 0.9 constant_dynamic-slice_fusion.2
  375.2 0.9 constant_dynamic-slice_fusion.2
  473.3 2.5 collective-permute-start.6
  475.8 3.2 collective-permute-start.5
  479.3 2.8 collective-permute-start.4
  482.8 4.7 collective-permute-done.4
  487.8 1.9 fusion.32
  (378 shorter events, 106.9 us)
Async XLA Ops:
  6.5 108.0 %copy-start = (bf16[1,4096,96]{1,2,0:T(8,128)(2,1)S(1)}, bf16[1,4096,96]{1,2,0:T(8,128)(2,1)}, u32[]{:S(2)}) copy-start(bf16[1,4096,96]{1,2,0:T(8,128)(2,1)} %param.15) | copy-start | bytes 2359300
  6.5 362.4 %all-gather.7.cloned.1.call-start = ((), (), s32[]{:S(2)}) async-start(), calls=%async_computation | async-start | bytes 8519680 | tf_op jit(solution)/shard_map/all_gather | solution.py:24
  6.5 13.6 %collective-permute-start.2 = (s32[1,16]{1,0:T(1,128)}, s32[1,16]{1,0:T(1,128)S(1)}, u32[]{:S(2)}, u32[]{:S(2)}) collective-permute-start(s32[1,16]{1,0:T(1,128)} %param.22), channel_id=1, source_target_pairs={{448,0},{0,64},{64,128},{128,192},{192,256},{256,320},{320,384},{3... | collective-permute-start | bytes 200 | tf_op jit(solution)/shard_map/ppermute | solution.py:20
  10.6 9.5 %collective-permute-start.1 = (s32[1,8]{1,0:T(1,128)}, s32[1,8]{1,0:T(1,128)S(1)}, u32[]{:S(2)}, u32[]{:S(2)}) collective-permute-start(s32[1,8]{1,0:T(1,128)} %param.23), channel_id=1, source_target_pairs={{448,0},{0,64},{64,128},{128,192},{192,256},{256,320},{320,384},{3... | collective-permute-start | bytes 104 | tf_op jit(solution)/shard_map/ppermute | solution.py:20
  13.8 6.6 %collective-permute-start = (bf16[1,8,64]{2,1,0:T(8,128)(2,1)}, bf16[1,8,64]{2,1,0:T(8,128)(2,1)S(1)}, u32[]{:S(2)}, u32[]{:S(2)}) collective-permute-start(bf16[1,8,64]{2,1,0:T(8,128)(2,1)} %param.13), channel_id=1, source_target_pairs={{448,0},{0,64},{64,128},{128,192},{192,256},{256,320},{320,384},{3... | collective-permute-start | bytes 3080 | tf_op jit(solution)/shard_map/ppermute | solution.py:20
  113.9 0.7 copy-start.3
  114.6 76.6 %copy-start.4 = (s32[1,8]{1,0:T(1,128)S(1)}, s32[1,8]{1,0:T(1,128)}, u32[]{:S(2)}) copy-start(s32[1,8]{1,0:T(1,128)} %param.23) | copy-start | bytes 100
  114.6 77.1 %copy-start.1 = (bf16[1,8,64,1024]{3,2,1,0:T(8,128)(2,1)S(1)}, bf16[1,8,64,1024]{3,2,1,0:T(8,128)(2,1)}, u32[]{:S(2)}) copy-start(bf16[1,8,64,1024]{3,2,1,0:T(8,128)(2,1)} %param.17) | copy-start | bytes 3145732
  188.1 3.9 copy-start.2
  188.3 5.6 %collective-permute-start.3 = (bf16[8,4096]{1,0:T(8,128)(2,1)S(1)}, bf16[8,4096]{1,0:T(8,128)(2,1)S(1)}, u32[]{:S(2)}, u32[]{:S(2)}) collective-permute-start(bf16[8,4096]{1,0:T(8,128)(2,1)S(1)} %maximum_bitcast_fusion), channel_id=1, source_target_pairs={{64,0},{128,64},{192,128},{256,192},{320,256},{384,320},{448,384},... | collective-permute-start | bytes 196616 | tf_op jit(solution)/shard_map/ppermute | solution.py:20
  473.3 8.9 %collective-permute-start.6 = (f32[8,8,4]{1,0,2:T(8,128)S(1)}, f32[8,8,4]{1,0,2:T(8,128)S(1)}, u32[]{:S(2)}, u32[]{:S(2)}) collective-permute-start(f32[8,8,4]{1,0,2:T(8,128)S(1)} %copy.96), channel_id=1, source_target_pairs={{448,0},{0,64},{64,128},{128,192},{192,256},{256,320},{320,384},{3... | collective-permute-start | bytes 3080 | tf_op jit(solution)/shard_map/ppermute | solution.py:20
  475.8 6.6 %collective-permute-start.5 = (f32[8,8,4]{1,0,2:T(8,128)S(1)}, f32[8,8,4]{1,0,2:T(8,128)S(1)}, u32[]{:S(2)}, u32[]{:S(2)}) collective-permute-start(f32[8,8,4]{1,0,2:T(8,128)S(1)} %copy.91), channel_id=1, source_target_pairs={{448,0},{0,64},{64,128},{128,192},{192,256},{256,320},{320,384},{3... | collective-permute-start | bytes 3080 | tf_op jit(solution)/shard_map/ppermute | solution.py:20
  479.3 8.2 %collective-permute-start.4 = (f32[8,8,4,128]{3,2,1,0:T(4,128)S(1)}, f32[8,8,4,128]{3,2,1,0:T(4,128)S(1)}, u32[]{:S(2)}, u32[]{:S(2)}) collective-permute-start(f32[8,8,4,128]{3,2,1,0:T(4,128)S(1)} %get-tuple-element.183), channel_id=1, source_target_pairs={{448,0},{0,64},{64,128},{128,192},{192,256},{256,320},{320,384},{3... | collective-permute-start | bytes 393224 | tf_op jit(solution)/shard_map/ppermute | solution.py:20
Sparse Core Ops, SparseCore 0:
  196.8 172.1 all-gather.6
where the time goes:
time: 498 us; the launch traced here: 497 us
  blocking collectives  316 us (63%)
  local copies, waits for them, and re-layouts  77.4 us (16%)
  other arithmetic  35 us (7%)
  waiting for transfers between devices  24.9 us (5%)
  starting transfers between devices  21.8 us (4%)
  between operations  13.6 us (3%)
  matrix products  5.92 us (1%)
    all_gather x2, blocking collectives, combined_all(): everything = jax.tree.map(lambda part: lax.all_gather(part, axis), array)  153 us
    all_gather x1, blocking collectives, local(): x_full = lax.all_gather(x_local, 'tp', axis=1, tiled=True)  91.1 us
    all_gather x1, blocking collectives, local(): query_key_value = lax.all_gather(qkv_local, 'tp', axis=1, tiled=True)  71.9 us
    dynamic_slice x63, local copies, waits for them, and re-layouts, hop(): return combine(so_far, jax.tree.map(lambda part: part[k], everything))  57.5 us
    add x63, other arithmetic, combine(): left[2] * scale_left[..., None] + right[2] * scale_right[..., None]  26.8 us
    ppermute x7, starting transfers between devices, passed_along(): return lax.ppermute(block, axis, route)  21.8 us
    all_gather x1, waiting for transfers between devices, combined_all(): everything = jax.tree.map(lambda part: lax.all_gather(part, axis), array)  18.3 us
  transfers between devices with their start and end apart: 8, of which 4 were waited for; matrix products, arithmetic and copies ran while one was open for 1% of the time, Pallas kernels for 0%

commit v1 on v0

v1 whole, which is shorter than its diff:
```python
import functools

import jax
import jax.numpy as jnp
import numpy as np
from jax import lax
from jax.experimental import pallas as pl
from jax.experimental.pallas import tpu as pltpu
from jax.sharding import PartitionSpec as P

MESH = pl.DeviceIdType.MESH
F32, BF16, I32 = jnp.float32, jnp.bfloat16, jnp.int32

ROWS = 8
HEAD = 128
QUERY_HEADS = 32
KEY_HEADS = 8
HEADS = QUERY_HEADS + 2 * KEY_HEADS
PAGE = 64
BLOCKS = 4
NEAR = 16
SLOTS = 8
TOKENS = SLOTS * PAGE
SCALE = 1.0 / HEAD**0.5
MASKED = -1e30
LOWEST = -1e25
ROPE_BASE = 500000.0
X_FAR, X_NEAR, Q_FAR, Q_NEAR, PART_NEAR, PART_FAR, OUT_NEAR = range(7)


def nt(left, right):
    return lax.dot_general(
        left, right, (((1,), (1,)), ((), ())), preferred_element_type=F32
    )


def thirds(value):
    first = value.astype(BF16).astype(F32)
    rest = value - first
    second = rest.astype(BF16).astype(F32)
    return first, second, rest - second


def pack_stats(top, total, shape):
    lane = lax.broadcasted_iota(I32, shape, 1)
    pieces = thirds(top) + thirds(total)
    tile = jnp.broadcast_to(pieces[5], shape)
    for k in range(4, -1, -1):
        tile = jnp.where(lane < 16 * (k + 1), jnp.broadcast_to(pieces[k], shape), tile)
    return tile.astype(BF16)


def unpack_stats(tile):
    wide = tile.astype(F32)
    part = [wide[:, 16 * k : 16 * k + 1] for k in range(6)]
    return part[0] + part[1] + part[2], part[3] + part[4] + part[5]


def merge(tops, totals, sums):
    top = functools.reduce(jnp.maximum, tops)
    total, weighted = 0.0, 0.0
    for t, l, a in zip(tops, totals, sums):
        factor = jnp.exp(t - top)
        total = total + factor * l
        weighted = weighted + factor * a
    return top, total, weighted


def kernel(
    x_hbm,
    gain_hbm,
    wq_hbm,
    wo_hbm,
    key_hbm,
    value_hbm,
    scale_hbm,
    owner_hbm,
    number_hbm,
    length_hbm,
    row_hbm,
    freq_hbm,
    out_ref,
    x_own,
    gain,
    wq,
    wo,
    keys,
    values,
    scales,
    owner,
    number,
    length,
    row,
    freq,
    bias,
    turn,
    x_send,
    x_far,
    x_pack,
    x_all,
    q_send,
    q_far,
    q_all,
    heads,
    part_send,
    part_all,
    sum_send,
    sum_all,
    att_send,
    att_all,
    local_sem,
    send_sem,
    recv_sem,
):
    section = lax.axis_index("section")
    tp = lax.axis_index("tp")
    block, mine = tp // NEAR, tp % NEAR
    sections = lax.axis_size("section")
    after = lax.rem(section + 1, sections)
    before = lax.rem(section + sections - 1, sections)

    def near(d):
        return lax.rem(mine + d, NEAR)

    def near_id(other):
        return {"tp": block * NEAR + other}

    def far_id(where, other):
        return {"section": where, "tp": other * NEAR + mine}

    barrier = pltpu.get_barrier_semaphore()

    def greet_near(d, carry):
        pl.semaphore_signal(barrier, inc=1, device_id=near_id(near(d)), device_id_type=MESH)
        return carry

    def greet_far(d, carry):
        other = lax.rem(block + d, BLOCKS)
        pl.semaphore_signal(barrier, inc=1, device_id=far_id(after, other), device_id_type=MESH)
        pl.semaphore_signal(barrier, inc=1, device_id=far_id(before, other), device_id_type=MESH)
        return carry

    lax.fori_loop(0, BLOCKS, greet_far, 0)
    lax.fori_loop(1, NEAR, greet_near, 0)

    moves = [
        pltpu.make_async_copy(src, dst, local_sem.at[k])
        for k, (src, dst) in enumerate(
            [
                (x_hbm, x_own),
                (row_hbm, row),
                (length_hbm, length),
                (owner_hbm, owner),
                (number_hbm, number),
                (scale_hbm, scales),
                (freq_hbm, freq),
                (key_hbm, keys),
                (value_hbm, values),
                (gain_hbm, gain),
                (wq_hbm, wq.at[pl.ds(0, 96)]),
                (wo_hbm, wo),
            ]
        )
    ]
    for move in moves:
        move.start()
    wq[96:128, :] = jnp.zeros((32, wq.shape[1]), BF16)

    moves[0].wait()
    x_here = x_own[...].astype(F32)
    x_send[...] = jnp.concatenate([x_here, x_here], axis=1).astype(BF16)

    for k in range(1, 7):
        moves[k].wait()
    lane = lax.broadcasted_iota(I32, (ROWS, HEAD), 1)
    sub = lax.broadcasted_iota(I32, (ROWS, HEAD), 0)
    low = lane < HEAD // 2
    row_of = jnp.zeros((ROWS, HEAD), I32)
    limit = jnp.zeros((ROWS, HEAD), I32)
    for r in range(ROWS):
        request = row[0, r]
        row_of = jnp.where(sub == r, request, row_of)
        limit = jnp.where(sub == r, length[0, request], limit)
    for j in range(SLOTS // 2):
        tok_owner = jnp.where(low, owner[0, 2 * j], owner[0, 2 * j + 1])
        tok_page = jnp.where(low, number[0, 2 * j], number[0, 2 * j + 1])
        tok_pos = tok_page * PAGE + lane % PAGE
        seen = (tok_owner == row_of) & (tok_pos < limit)
        bias[:, HEAD * j : HEAD * (j + 1)] = jnp.where(seen, 0.0, MASKED)
    angle = limit.astype(F32) * freq[...]
    turn[0] = jnp.cos(angle)
    sine = jnp.sin(angle)
    turn[1] = jnp.where(low, -sine, sine)

    moves[7].wait()
    moves[8].wait()

    def restore(k, carry):
        at = pl.ds(pl.multiple_of(k * PAGE, PAGE), PAGE)
        both = scales[k]
        for which, store in ((0, keys), (1, values)):
            for g in range(KEY_HEADS):
                cols = pl.ds(g * HEAD, HEAD)
                factor = jnp.broadcast_to(both[which : which + 1, g : g + 1], (PAGE, HEAD))
                store[at, cols] = (store[at, cols].astype(F32) * factor).astype(BF16)
        return carry

    lax.fori_loop(0, SLOTS, restore, 0)
    moves[9].wait()
    moves[10].wait()
    moves[11].wait()

    def start_far(stage, where, src, dst):
        def go(d, carry):
            other = lax.rem(block + BLOCKS // 2 + d, BLOCKS)
            pltpu.make_async_remote_copy(
                src_ref=src,
                dst_ref=dst.at[block],
                send_sem=send_sem.at[stage],
                recv_sem=recv_sem.at[stage],
                device_id=far_id(where, other),
                device_id_type=MESH,
            ).start()
            return carry

        lax.fori_loop(0, BLOCKS, go, 0)

    def start_near(stage, src_of, dst):
        def go(d, carry):
            other = near(d)
            pltpu.make_async_remote_copy(
                src_ref=src_of(other),
                dst_ref=dst.at[mine],
                send_sem=send_sem.at[stage],
                recv_sem=recv_sem.at[stage],
                device_id=near_id(other),
                device_id_type=MESH,
            ).start()
            return carry

        lax.fori_loop(1, NEAR, go, 0)

    def all_of(stage, part):
        return pltpu.make_async_remote_copy(
            src_ref=part,
            dst_ref=part,
            send_sem=send_sem.at[stage],
            recv_sem=recv_sem.at[stage],
            device_id=near_id(near(1)),
            device_id_type=MESH,
        )

    far_waits = {
        X_FAR: x_far,
        Q_FAR: q_far,
        PART_FAR: sum_all,
        X_NEAR: x_all.at[pl.ds(0, NEAR - 1)],
        Q_NEAR: q_all.at[pl.ds(0, NEAR - 1)],
        PART_NEAR: part_all.at[pl.ds(0, NEAR - 1)],
        OUT_NEAR: att_all.at[pl.ds(0, NEAR - 1)],
    }

    def arrived(stage):
        all_of(stage, far_waits[stage]).wait_recv()

    pl.semaphore_wait(barrier, NEAR - 1 + 2 * BLOCKS)

    start_far(X_FAR, after, x_send, x_far)
    arrived(X_FAR)
    for u in range(2):
        tile = jnp.where(low, x_far[2 * u].astype(F32), x_far[2 * u + 1].astype(F32))
        x_pack[u] = tile.astype(BF16)
    x_all[mine] = x_pack[...]
    start_near(X_NEAR, lambda other: x_pack, x_all)
    arrived(X_NEAR)

    tiles = [None] * 32
    square = jnp.zeros((ROWS, HEAD), F32)
    for j in range(NEAR // 2):
        for u in range(2):
            even = x_all[2 * j, u].astype(F32)
            odd = x_all[2 * j + 1, u].astype(F32)
            square = square + even * even + odd * odd
            tiles[16 * u + j] = jnp.where(low, even, pltpu.roll(odd, 64, 1))
            tiles[16 * u + 8 + j] = jnp.where(low, pltpu.roll(even, 64, 1), odd)
    mean = jnp.sum(square, axis=1, keepdims=True) * (1.0 / 4096)
    shrink = lax.rsqrt(mean + 1e-05)
    normed = jnp.concatenate(
        [
            (tiles[t] * shrink * gain[:, HEAD * t : HEAD * (t + 1)]).astype(BF16)
            for t in range(32)
        ],
        axis=1,
    )
    columns = nt(normed, wq[...])
    place = tp % 4
    turned = columns
    for k in range(1, 4):
        turned = jnp.where(place == k, pltpu.roll(columns, 96 * k % 128, 1), turned)
    q_send[...] = turned.astype(BF16)

    start_far(Q_FAR, before, q_send, q_far)
    arrived(Q_FAR)
    q_all[mine] = q_far[...]
    start_near(Q_NEAR, lambda other: q_far, q_all)
    arrived(Q_NEAR)

    cosine, sine = turn[0], turn[1]
    for c in range(BLOCKS):
        for plane in range(4):
            b = [q_all[4 * plane + p, c].astype(F32) for p in range(4)]
            for k, edge in enumerate((96, 64, 32)):
                h = 3 * (4 * c + plane) + k
                head = jnp.where(lane < edge, b[k], b[k + 1])
                if h < QUERY_HEADS + KEY_HEADS:
                    head = head * cosine + pltpu.roll(head, 64, 1) * sine
                    head = head.astype(BF16).astype(F32)
                heads[h] = head

    hidden = jnp.concatenate([bias[...]] * 4, axis=0)
    for g in range(KEY_HEADS):
        cols = slice(g * HEAD, (g + 1) * HEAD)
        query = jnp.concatenate([heads[4 * g + k] for k in range(4)], axis=0).astype(BF16)
        score = nt(query, keys[:, cols]) * SCALE + hidden
        top = jnp.maximum(jnp.max(score, axis=1, keepdims=True), LOWEST)
        weight = jnp.exp(score - top)
        total = jnp.sum(weight, axis=1, keepdims=True)
        weighted = jnp.dot(
            weight.astype(BF16), values[:, cols], preferred_element_type=F32
        ).astype(BF16)
        stats = pack_stats(top, total, (4 * ROWS, HEAD))
        for k in range(2):
            part_send[2 * g + k, 0] = weighted[16 * k : 16 * (k + 1)]
            part_send[2 * g + k, 1] = stats[16 * k : 16 * (k + 1)]

    start_near(PART_NEAR, lambda other: part_send.at[other], part_all)
    part_all[mine] = part_send[mine]
    own_query = jnp.concatenate([heads[2 * mine], heads[2 * mine + 1]], axis=0)
    own_key = heads[QUERY_HEADS + mine // 2]
    own_value = heads[QUERY_HEADS + KEY_HEADS + mine // 2]
    own_score = (
        jnp.sum(own_query * jnp.concatenate([own_key] * 2, axis=0), axis=1, keepdims=True) * SCALE
    )
    own_score = jnp.where(block == 0, own_score, MASKED)
    arrived(PART_NEAR)
    stats = [unpack_stats(part_all[i, 1]) for i in range(NEAR)]
    top, total, weighted = merge(
        [s[0] for s in stats] + [own_score],
        [s[1] for s in stats] + [jnp.ones_like(own_score)],
        [part_all[i, 0].astype(F32) for i in range(NEAR)]
        + [jnp.concatenate([own_value] * 2, axis=0)],
    )
    sum_send[0] = weighted.astype(BF16)
    sum_send[1] = pack_stats(top, total, (2 * ROWS, HEAD))

    start_far(PART_FAR, after, sum_send, sum_all)
    arrived(PART_FAR)
    stats = [unpack_stats(sum_all[c, 1]) for c in range(BLOCKS)]
    top, total, weighted = merge(
        [s[0] for s in stats],
        [s[1] for s in stats],
        [sum_all[c, 0].astype(F32) for c in range(BLOCKS)],
    )
    att_send[...] = (weighted / total).astype(BF16)
    att_all[mine] = att_send[...]
    start_near(OUT_NEAR, lambda other: att_send, att_all)
    arrived(OUT_NEAR)
    pieces = []
    for i in range(NEAR):
        pair = att_all[i].astype(F32)
        pieces += [pair[:ROWS], pair[ROWS:]]
    attended = jnp.concatenate(pieces, axis=1).astype(BF16)
    out_ref[...] = nt(attended, wo[...]) + x_far[block].astype(F32)[:, :64]

    for stage, part in far_waits.items():
        all_of(stage, part).wait_send()


def local(x, gain, wq, wo, key_codes, value_codes, scale_table, owner, number, lengths, rows):
    half = HEAD // 2
    freq = ROPE_BASE ** (-np.arange(half, dtype=np.float64) / half)
    freq = jnp.asarray(np.concatenate([freq, freq]).astype(np.float32)[None, :])
    operands = (
        x[0],
        gain,
        jnp.swapaxes(wq[0], 0, 1),
        jnp.swapaxes(wo[0], 0, 1),
        key_codes[0].reshape(TOKENS, KEY_HEADS * HEAD),
        value_codes[0].reshape(TOKENS, KEY_HEADS * HEAD),
        scale_table[0],
        owner,
        number,
        lengths,
        rows,
        freq,
    )
    vmem, smem = pltpu.VMEM, pltpu.SMEM
    out = pl.pallas_call(
        kernel,
        out_shape=jax.ShapeDtypeStruct((ROWS, 64), F32),
        in_specs=[pl.BlockSpec(memory_space=pl.ANY)] * len(operands),
        out_specs=pl.BlockSpec(memory_space=pltpu.VMEM),
        scratch_shapes=[
            vmem((ROWS, 64), BF16),
            vmem((1, 4096), F32),
            vmem((128, 4096), BF16),
            vmem((64, 4096), BF16),
            vmem((TOKENS, 1024), BF16),
            vmem((TOKENS, 1024), BF16),
            vmem((SLOTS, 2, KEY_HEADS), F32),
            smem((1, SLOTS), I32),
            smem((1, SLOTS), I32),
            smem((1, 16), I32),
            smem((1, ROWS), I32),
            vmem((1, HEAD), F32),
            vmem((ROWS, TOKENS), F32),
            vmem((2, ROWS, HEAD), F32),
            vmem((ROWS, HEAD), BF16),
            vmem((BLOCKS, ROWS, HEAD), BF16),
            vmem((2, ROWS, HEAD), BF16),
            vmem((NEAR, 2, ROWS, HEAD), BF16),
            vmem((ROWS, HEAD), BF16),
            vmem((BLOCKS, ROWS, HEAD), BF16),
            vmem((NEAR, BLOCKS, ROWS, HEAD), BF16),
            vmem((HEADS, ROWS, HEAD), F32),
            vmem((NEAR, 2, 2 * ROWS, HEAD), BF16),
            vmem((NEAR, 2, 2 * ROWS, HEAD), BF16),
            vmem((2, 2 * ROWS, HEAD), BF16),
            vmem((BLOCKS, 2, 2 * ROWS, HEAD), BF16),
            vmem((2 * ROWS, HEAD), BF16),
            vmem((NEAR, 2 * ROWS, HEAD), BF16),
            pltpu.SemaphoreType.DMA((12,)),
            pltpu.SemaphoreType.DMA((7,)),
            pltpu.SemaphoreType.DMA((7,)),
        ],
        compiler_params=pltpu.CompilerParams(
            collective_id=0, has_side_effects=True, vmem_limit_bytes=32 * 2**20
        ),
    )(*operands)
    return out[None]


def solution(mesh):
    in_specs = (
        P("section", None, "tp"),
        P("section", None),
        P("section", None, "tp"),
        P("section", None, "tp"),
        P("section", "tp", None, None),
        P("section", "tp", None, None),
        P("section", "tp", None, None),
        P("section", "tp"),
        P("section", "tp"),
        P("section", None),
        P("section", None),
    )
    out_specs = P("section", None, "tp")
    return jax.shard_map(local, mesh=mesh, in_specs=in_specs, out_specs=out_specs, check_vma=False)
```

time: 498 us -> 75.2 us (0.15)
  blocking collectives: 316 us -> 0 us
  local copies, waits for them, and re-layouts: 77.4 us -> 8.59 us
  Pallas kernels: 0 us -> 66.2 us
  other arithmetic: 35 us -> 0 us
  waiting for transfers between devices: 24.9 us -> 0 us
  starting transfers between devices: 21.8 us -> 0 us
  between operations: 13.6 us -> 0.03 us
  matrix products: 5.92 us -> 0 us
    all_gather x4 -> x0, blocking collectives: 316 us -> none  [the longest x2 153 us: combined_all(): everything = jax.tree.map(lambda part: lax.all_gather(part, axis), array)]
    pallas_call x0 -> x1, Pallas kernels: none -> 66.2 us  [local(): pl.pallas_call(kernel, out_shape=jax.ShapeDtypeStruct((ROWS, 64), F32), i...]
    dynamic_slice x63 -> x0, local copies, waits for them, and re-layouts: 57.5 us -> none  [hop(): return combine(so_far, jax.tree.map(lambda part: part[k], everything))]
    add x128 -> x0, other arithmetic: 29.3 us -> none  [the longest x63 26.8 us: combine(): left[2] * scale_left[..., None] + right[2] * scale_right[..., None]]
    ppermute x7 -> x0, starting transfers between devices: 21.8 us -> none  [passed_along(): return lax.ppermute(block, axis, route)]
    all_gather x1 -> x0, waiting for transfers between devices: 18.3 us -> none  [combined_all(): everything = jax.tree.map(lambda part: lax.all_gather(part, axis), array)]
    exp x128 -> x0, local copies, waits for them, and re-layouts: 15.5 us -> none  [the longest x63 7.63 us: combine(): scale_right = jnp.exp(right[0] - top)]
    unnamed x14 -> x25, local copies, waits for them, and re-layouts: 1.57 us -> 8.59 us
  transfers between devices with their start and end apart: 8 -> 0, of which waited for: 4 -> 0; matrix products, arithmetic and copies ran while one was open for 1% -> 0% of each run, Pallas kernels for 0% -> 0%
where the time goes in v1:
time: 75.2 us; the launch traced here: 74.8 us
  Pallas kernels  66.2 us (88%)
  local copies, waits for them, and re-layouts  8.59 us (11%)
    pallas_call x1, Pallas kernels, local(): pl.pallas_call(kernel, out_shape=jax.ShapeDtypeStruct((ROWS, 64), F32), i...  66.2 us
    unnamed x25, local copies, waits for them, and re-layouts  8.59 us

profile of v1, /device:TPU:1, one launch (start us, length us, event | category | flops | bytes accessed | tf_op | source)
XLA Modules:
  0.0 74.8 jit_solution(13033586488827506135)
XLA Ops:
  0.0 0.0 copy-start.5
  0.0 0.0 copy-start.6
  0.0 0.0 copy-start.8
  0.0 0.7 copy-done.5
  0.7 0.0 copy-done.6
  0.7 0.0 copy-done.7
  0.7 0.0 copy-done.8
  0.7 0.0 copy-start
  0.7 1.2 %copy-done = bf16[1,8,64,1024]{3,2,1,0:T(8,128)(2,1)S(1)} copy-done((bf16[1,8,64,1024]{3,2,1,0:T(8,128)(2,1)S(1)}, bf16[1,8,64,1024]{3,2,1,0:T(8,128)(2,1)}, u32[]{:S(2)}) %copy-start) | copy-done | bytes 1048600
  1.9 0.0 copy-start.1
  1.9 1.2 %copy-done.1 = bf16[1,8,64,1024]{3,2,1,0:T(8,128)(2,1)S(1)} copy-done((bf16[1,8,64,1024]{3,2,1,0:T(8,128)(2,1)S(1)}, bf16[1,8,64,1024]{3,2,1,0:T(8,128)(2,1)}, u32[]{:S(2)}) %copy-start.1) | copy-done | bytes 1048600
  3.2 0.0 copy-start.2
  3.2 1.1 %copy-done.2 = bf16[1,4096,96]{1,2,0:T(8,128)(2,1)S(1)} copy-done((bf16[1,4096,96]{1,2,0:T(8,128)(2,1)S(1)}, bf16[1,4096,96]{1,2,0:T(8,128)(2,1)}, u32[]{:S(2)}) %copy-start.2) | copy-done | bytes 786456
  4.3 0.0 copy-start.3
  4.3 1.0 %copy-done.3 = bf16[1,4096,64]{1,2,0:T(8,128)(2,1)S(1)} copy-done((bf16[1,4096,64]{1,2,0:T(8,128)(2,1)S(1)}, bf16[1,4096,64]{1,2,0:T(8,128)(2,1)}, u32[]{:S(2)}) %copy-start.3) | copy-done | bytes 524312
  5.3 0.0 copy-start.4
  5.3 0.7 copy-done.4
  6.1 0.0 copy-start.9
  6.1 0.7 copy-done.9
  6.7 0.0 copy-start.10
  6.7 0.7 copy-done.10
  7.4 0.7 copy-done.11
  8.0 66.2 %shard_map.118 = f32[8,64]{1,0:T(8,128)S(1)} custom-call(bf16[8,64]{1,0:T(8,128)(2,1)S(1)} %bitcast.17, f32[1,4096]{1,0:T(1,128)S(1)} %copy-done.4, bf16[96,4096]{1,0:T(8,128)(2,1)S(1)} %bitcast.13, bf16[64,4096]{1,0:T(8,128)(2,1)S(1)} %bitcast.14, bf16[512,1024]{1,0:T(8,128)(2,1)S(1)} %bitcast.11, bf16[512,1024]{1,0:T(8,128)(2,1)S(1)} %bitcast.12, ...), custom_call_target="tpu_custom_call" | custom-call | tf_op jit(solution)/shard_map/pallas_call | solution.py:398
  74.2 0.6 copy.17
  (2 shorter events, 0.0 us)
Async XLA Ops:
  0.0 0.7 copy-start.5
  0.0 0.7 copy-start.6
  0.0 0.7 copy-start.7
  0.0 0.7 copy-start.8
  0.7 1.2 %copy-start = (bf16[1,8,64,1024]{3,2,1,0:T(8,128)(2,1)S(1)}, bf16[1,8,64,1024]{3,2,1,0:T(8,128)(2,1)}, u32[]{:S(2)}) copy-start(bf16[1,8,64,1024]{3,2,1,0:T(8,128)(2,1)} %param.16) | copy-start | bytes 3145732
  1.9 1.2 %copy-start.1 = (bf16[1,8,64,1024]{3,2,1,0:T(8,128)(2,1)S(1)}, bf16[1,8,64,1024]{3,2,1,0:T(8,128)(2,1)}, u32[]{:S(2)}) copy-start(bf16[1,8,64,1024]{3,2,1,0:T(8,128)(2,1)} %param.17) | copy-start | bytes 3145732
  3.2 1.1 %copy-start.2 = (bf16[1,4096,96]{1,2,0:T(8,128)(2,1)S(1)}, bf16[1,4096,96]{1,2,0:T(8,128)(2,1)}, u32[]{:S(2)}) copy-start(bf16[1,4096,96]{1,2,0:T(8,128)(2,1)} %param.14) | copy-start | bytes 2359300
  4.3 1.0 %copy-start.3 = (bf16[1,4096,64]{1,2,0:T(8,128)(2,1)S(1)}, bf16[1,4096,64]{1,2,0:T(8,128)(2,1)}, u32[]{:S(2)}) copy-start(bf16[1,4096,64]{1,2,0:T(8,128)(2,1)} %param.15) | copy-start | bytes 1572868
  5.3 0.7 copy-start.4
  6.1 0.7 copy-start.9
  6.7 0.7 copy-start.10
  7.4 0.7 copy-start.11

commit v2 on v1

v2 whole, which is shorter than its diff:
```python
import functools

import jax
import jax.numpy as jnp
import numpy as np
from jax import lax
from jax.experimental import pallas as pl
from jax.experimental.pallas import tpu as pltpu
from jax.sharding import PartitionSpec as P

MESH = pl.DeviceIdType.MESH
F32, BF16, I32 = jnp.float32, jnp.bfloat16, jnp.int32

ROWS = 8
HEAD = 128
QUERY_HEADS = 32
KEY_HEADS = 8
HEADS = QUERY_HEADS + 2 * KEY_HEADS
PAGE = 64
BLOCKS = 4
PLANES = 16
NEAR = 16
SLOTS = 8
TOKENS = SLOTS * PAGE
SCALE = 1.0 / HEAD**0.5
MASKED = -1e30
LOWEST = -1e25
ROPE_BASE = 500000.0
FARTHEST_FIRST = (7, 5, 3, 6, 1, 4, 2, 0)
TOGETHER = 2
X_LINE, X_PLANE, Q_LINE, Q_PLANE, PART_NEAR, PART_FAR, OUT_NEAR = range(7)


def nt(left, right):
    return lax.dot_general(
        left, right, (((1,), (1,)), ((), ())), preferred_element_type=F32
    )


def thirds(value):
    first = value.astype(BF16).astype(F32)
    rest = value - first
    second = rest.astype(BF16).astype(F32)
    return first, second, rest - second


def pack_stats(top, total, low, lane):
    slot = lane % (HEAD // 2) // 8
    pieces = thirds(top) + thirds(total)
    tiles = []
    for at in range(0, top.shape[0], 2 * ROWS):
        tile = jnp.zeros(lane.shape, F32)
        for k, piece in enumerate(pieces):
            pair = jnp.where(low, piece[at : at + ROWS], piece[at + ROWS : at + 2 * ROWS])
            tile = jnp.where(slot == k, pair, tile)
        tiles.append(tile.astype(BF16))
    return tiles


def unpack_stats(tile):
    wide = tile.astype(F32)
    part = [
        jnp.concatenate([wide[:, at : at + 1], wide[:, at + 64 : at + 65]], axis=0)
        for at in range(0, 48, 8)
    ]
    return part[0] + part[1] + part[2], part[3] + part[4] + part[5]


def both(parts):
    return jnp.concatenate([parts[0].astype(F32), parts[1].astype(F32)], axis=0)


def merge(tops, totals, sums):
    top = functools.reduce(jnp.maximum, tops)
    total, weighted = 0.0, 0.0
    for t, l, a in zip(tops, totals, sums):
        factor = jnp.exp(t - top)
        total = total + factor * l
        weighted = weighted + factor * a
    return top, total, weighted


def kernel(
    x_hbm,
    gain_hbm,
    wq_hbm,
    wo_hbm,
    key_hbm,
    value_hbm,
    scale_hbm,
    owner_hbm,
    number_hbm,
    length_hbm,
    row_hbm,
    freq_hbm,
    out_ref,
    x_own,
    gain,
    wq,
    wo,
    keys,
    values,
    scales,
    owner,
    number,
    length,
    row,
    freq,
    bias,
    turn,
    x_send,
    x_line,
    x_pack,
    x_all,
    q_send,
    q_line,
    q_all,
    heads,
    part_send,
    part_all,
    sum_send,
    sum_all,
    att_send,
    att_all,
    local_sem,
    send_sem,
    recv_sem,
):
    section = lax.axis_index("section")
    tp = lax.axis_index("tp")
    block, mine = tp // NEAR, tp % NEAR
    plane, place = tp // 4, tp % 4
    sections = lax.axis_size("section")
    after = lax.rem(section + 1, sections)
    before = lax.rem(section + sections - 1, sections)

    def near(d):
        return lax.rem(mine + d, NEAR)

    def near_id(other):
        return {"tp": block * NEAR + other}

    def far_id(where, other):
        return {"section": where, "tp": other * NEAR + mine}

    def line_id(other):
        return {"tp": other * 4 + place}

    def plane_id(where, other):
        return {"section": where, "tp": plane * 4 + other}

    barrier = pltpu.get_barrier_semaphore()

    def greet(device):
        pl.semaphore_signal(barrier, inc=1, device_id=device, device_id_type=MESH)

    def greet_line(k, carry):
        greet(line_id(lax.rem(plane + k, PLANES)))
        return carry

    def greet_shift(k, carry):
        for where in (before, after):
            greet(plane_id(where, k))
        return carry

    def greet_far(k, carry):
        other = lax.rem(block + k, BLOCKS)
        for where in (before, after):
            greet(far_id(where, other))
        return carry

    def greet_near(k, carry):
        @pl.when(lax.rem(mine + k, 4) != place)
        def _():
            greet(near_id(near(k)))

        return carry

    lax.fori_loop(1, PLANES, greet_line, 0)
    lax.fori_loop(0, 4, greet_shift, 0)
    lax.fori_loop(1, BLOCKS, greet_far, 0)
    lax.fori_loop(1, NEAR, greet_near, 0)
    greetings = PLANES - 1 + 8 + 2 * (BLOCKS - 1) + NEAR - 4

    moves = [
        pltpu.make_async_copy(src, dst, local_sem.at[k])
        for k, (src, dst) in enumerate(
            [
                (x_hbm, x_own),
                (row_hbm, row),
                (length_hbm, length),
                (owner_hbm, owner),
                (number_hbm, number),
                (scale_hbm, scales),
                (freq_hbm, freq),
                (key_hbm, keys),
                (value_hbm, values),
                (gain_hbm, gain),
                (wq_hbm, wq.at[pl.ds(0, 96)]),
                (wo_hbm, wo),
            ]
        )
    ]
    for move in moves:
        move.start()
    wq[96:128, :] = jnp.zeros((32, wq.shape[1]), BF16)

    moves[0].wait()
    x_here = x_own[...].astype(F32)
    x_send[...] = jnp.concatenate([x_here, x_here], axis=1).astype(BF16)

    lane = lax.broadcasted_iota(I32, (ROWS, HEAD), 1)
    low = lane < HEAD // 2

    def prepare():
        for k in range(1, 7):
            moves[k].wait()
        sub = lax.broadcasted_iota(I32, (ROWS, HEAD), 0)
        row_of = jnp.zeros((ROWS, HEAD), I32)
        limit = jnp.zeros((ROWS, HEAD), I32)
        for r in range(ROWS):
            request = row[0, r]
            row_of = jnp.where(sub == r, request, row_of)
            limit = jnp.where(sub == r, length[0, request], limit)
        for j in range(SLOTS // 2):
            tok_owner = jnp.where(low, owner[0, 2 * j], owner[0, 2 * j + 1])
            tok_page = jnp.where(low, number[0, 2 * j], number[0, 2 * j + 1])
            tok_pos = tok_page * PAGE + lane % PAGE
            seen = (tok_owner == row_of) & (tok_pos < limit)
            bias[:, HEAD * j : HEAD * (j + 1)] = jnp.where(seen, 0.0, MASKED)
        angle = limit.astype(F32) * freq[...]
        turn[0] = jnp.cos(angle)
        sine = jnp.sin(angle)
        turn[1] = jnp.where(low, -sine, sine)

        moves[7].wait()
        moves[8].wait()

        def restore(k, carry):
            at = pl.ds(pl.multiple_of(k * PAGE, PAGE), PAGE)
            both = scales[k]
            for which, store in ((0, keys), (1, values)):
                for g in range(KEY_HEADS):
                    cols = pl.ds(g * HEAD, HEAD)
                    factor = jnp.broadcast_to(both[which : which + 1, g : g + 1], (PAGE, HEAD))
                    store[at, cols] = (store[at, cols].astype(F32) * factor).astype(BF16)
            return carry

        lax.fori_loop(0, SLOTS, restore, 0)
        moves[9].wait()
        moves[10].wait()
        moves[11].wait()

    def send(stage, src, dst, device):
        pltpu.make_async_remote_copy(
            src_ref=src,
            dst_ref=dst,
            send_sem=send_sem.at[stage],
            recv_sem=recv_sem.at[stage],
            device_id=device,
            device_id_type=MESH,
        ).start()

    def start_far(stage, where, src, dst):
        def go(d, carry):
            other = lax.rem(block + BLOCKS // 2 + d, BLOCKS)
            send(stage, src, dst.at[block], far_id(where, other))
            return carry

        lax.fori_loop(0, BLOCKS, go, 0)

    def start_near(stage, src, dst):
        def go(d, carry):
            send(stage, src, dst.at[mine], near_id(near(d)))
            return carry

        lax.fori_loop(1, NEAR, go, 0)

    def start_line(stage, src, dst):
        half = PLANES // 2
        send(stage, src, dst.at[plane], line_id(lax.rem(plane + half, PLANES)))

        def go(d, carry):
            for shift in (half - d, half + d):
                send(stage, src, dst.at[plane], line_id(lax.rem(plane + shift, PLANES)))
            return carry

        lax.fori_loop(1, half, go, 0)

    def start_plane(stage, where, src, dst):
        def go(d, carry):
            send(stage, src, dst.at[place], plane_id(where, lax.rem(place + 3 - d, 4)))
            return carry

        lax.fori_loop(0, 4, go, 0)

    def all_of(stage, part):
        return pltpu.make_async_remote_copy(
            src_ref=part,
            dst_ref=part,
            send_sem=send_sem.at[stage],
            recv_sem=recv_sem.at[stage],
            device_id=near_id(near(1)),
            device_id_type=MESH,
        )

    expected = {
        X_LINE: x_line.at[pl.ds(0, PLANES - 1)],
        X_PLANE: x_all,
        Q_LINE: q_line.at[pl.ds(0, PLANES - 1)],
        Q_PLANE: q_all,
        PART_NEAR: part_all.at[pl.ds(0, NEAR - 1)],
        PART_FAR: sum_all,
        OUT_NEAR: att_all.at[pl.ds(0, NEAR - 1)],
    }

    def arrived(stage):
        all_of(stage, expected[stage]).wait_recv()

    early = plane < PLANES // 2
    pl.when(early)(prepare)
    pl.semaphore_wait(barrier, greetings)

    start_line(X_LINE, x_send, x_line)
    x_line[plane] = x_send[...]
    pl.when(jnp.logical_not(early))(prepare)
    arrived(X_LINE)
    for u in range(PLANES // 2):
        tile = jnp.where(low, x_line[2 * u].astype(F32), x_line[2 * u + 1].astype(F32))
        x_pack[u] = tile.astype(BF16)
    start_plane(X_PLANE, after, x_pack, x_all)
    arrived(X_PLANE)

    tiles = [None] * 32
    square = jnp.zeros((ROWS, HEAD), F32)
    for u in range(PLANES // 2):
        for j in range(2):
            even = x_all[2 * j, u].astype(F32)
            odd = x_all[2 * j + 1, u].astype(F32)
            square = square + even * even + odd * odd
            tiles[4 * u + j] = jnp.where(low, even, pltpu.roll(odd, 64, 1))
            tiles[4 * u + 2 + j] = jnp.where(low, pltpu.roll(even, 64, 1), odd)
    mean = jnp.sum(square, axis=1, keepdims=True) * (1.0 / 4096)
    shrink = lax.rsqrt(mean + 1e-05)
    normed = jnp.concatenate(
        [
            (tiles[t] * shrink * gain[:, HEAD * t : HEAD * (t + 1)]).astype(BF16)
            for t in range(32)
        ],
        axis=1,
    )
    columns = nt(normed, wq[...])
    turned = columns
    for k in range(1, 4):
        turned = jnp.where(place == k, pltpu.roll(columns, 96 * k % 128, 1), turned)
    q_send[...] = turned.astype(BF16)

    start_line(Q_LINE, q_send, q_line)
    q_line[plane] = q_send[...]
    arrived(Q_LINE)
    start_plane(Q_PLANE, before, q_line, q_all)
    arrived(Q_PLANE)

    cosine, sine = turn[0], turn[1]
    for z in range(PLANES):
        b = [q_all[p, z].astype(F32) for p in range(4)]
        for k, edge in enumerate((96, 64, 32)):
            head = jnp.where(lane < edge, b[k], b[k + 1])
            if 3 * z + k < QUERY_HEADS + KEY_HEADS:
                head = head * cosine + pltpu.roll(head, 64, 1) * sine
                head = head.astype(BF16).astype(F32)
            heads[3 * z + k] = head

    hidden = jnp.concatenate([bias[...]] * 4, axis=0)
    chip = mine // 2
    for at in range(0, len(FARTHEST_FIRST), TOGETHER):
        steps = FARTHEST_FIRST[at : at + TOGETHER]
        groups = [chip ^ k for k in steps]
        cols = [pl.ds(pl.multiple_of(g * HEAD, HEAD), HEAD) for g in groups]
        queries = [heads[pl.ds(4 * g, 4)].reshape(4 * ROWS, HEAD).astype(BF16) for g in groups]
        scores = [nt(q, keys[:, c]) * SCALE + hidden for q, c in zip(queries, cols)]
        tops = [jnp.maximum(jnp.max(s, axis=1, keepdims=True), LOWEST) for s in scores]
        weights = [jnp.exp(s - t) for s, t in zip(scores, tops)]
        sums = [
            jnp.dot(w.astype(BF16), values[:, c], preferred_element_type=F32).astype(BF16)
            for w, c in zip(weights, cols)
        ]
        totals = [jnp.sum(w, axis=1, keepdims=True) for w in weights]
        for n, g in enumerate(groups):
            first, second = pack_stats(tops[n], totals[n], low, lane)
            for core, stats in ((0, first), (1, second)):
                part_send[2 * g + core, 0] = sums[n][16 * core : 16 * core + 8]
                part_send[2 * g + core, 1] = sums[n][16 * core + 8 : 16 * core + 16]
                part_send[2 * g + core, 2] = stats
        for k, g in zip(steps, groups):
            if k:
                for other in (2 * g, 2 * g + 1):
                    send(PART_NEAR, part_send.at[other], part_all.at[mine], near_id(other))
    sibling = mine + 1 - 2 * (mine % 2)
    send(PART_NEAR, part_send.at[sibling], part_all.at[mine], near_id(sibling))
    part_all[mine] = part_send[mine]
    own_query = jnp.concatenate([heads[2 * mine], heads[2 * mine + 1]], axis=0)
    own_key = heads[QUERY_HEADS + mine // 2]
    own_value = heads[QUERY_HEADS + KEY_HEADS + mine // 2]
    own_score = (
        jnp.sum(own_query * jnp.concatenate([own_key] * 2, axis=0), axis=1, keepdims=True) * SCALE
    )
    own_score = jnp.where(block == 0, own_score, MASKED)
    arrived(PART_NEAR)
    stats = [unpack_stats(part_all[i, 2]) for i in range(NEAR)]
    top, total, weighted = merge(
        [s[0] for s in stats] + [own_score],
        [s[1] for s in stats] + [jnp.ones_like(own_score)],
        [both(part_all[i]) for i in range(NEAR)]
        + [jnp.concatenate([own_value] * 2, axis=0)],
    )
    sum_send[0] = weighted[:ROWS].astype(BF16)
    sum_send[1] = weighted[ROWS:].astype(BF16)
    sum_send[2] = pack_stats(top, total, low, lane)[0]

    start_far(PART_FAR, after, sum_send, sum_all)
    arrived(PART_FAR)
    stats = [unpack_stats(sum_all[c, 2]) for c in range(BLOCKS)]
    top, total, weighted = merge(
        [s[0] for s in stats],
        [s[1] for s in stats],
        [both(sum_all[c]) for c in range(BLOCKS)],
    )
    att_send[...] = (weighted / total).astype(BF16)
    att_all[mine] = att_send[...]
    start_near(OUT_NEAR, att_send, att_all)
    arrived(OUT_NEAR)
    pieces = []
    for i in range(NEAR):
        pair = att_all[i].astype(F32)
        pieces += [pair[:ROWS], pair[ROWS:]]
    attended = jnp.concatenate(pieces, axis=1).astype(BF16)
    x_here = x_all[place, plane // 2].astype(F32)
    x_here = jnp.where(plane % 2 == 0, x_here, pltpu.roll(x_here, 64, 1))[:, :64]
    out_ref[...] = nt(attended, wo[...]) + x_here

    for stage, part in expected.items():
        all_of(stage, part).wait_send()


def local(x, gain, wq, wo, key_codes, value_codes, scale_table, owner, number, lengths, rows):
    half = HEAD // 2
    freq = ROPE_BASE ** (-np.arange(half, dtype=np.float64) / half)
    freq = jnp.asarray(np.concatenate([freq, freq]).astype(np.float32)[None, :])
    operands = (
        x[0],
        gain,
        jnp.swapaxes(wq[0], 0, 1),
        jnp.swapaxes(wo[0], 0, 1),
        key_codes[0].reshape(TOKENS, KEY_HEADS * HEAD),
        value_codes[0].reshape(TOKENS, KEY_HEADS * HEAD),
        scale_table[0],
        owner,
        number,
        lengths,
        rows,
        freq,
    )
    vmem, smem = pltpu.VMEM, pltpu.SMEM
    out = pl.pallas_call(
        kernel,
        out_shape=jax.ShapeDtypeStruct((ROWS, 64), F32),
        in_specs=[pl.BlockSpec(memory_space=pltpu.HBM)] * len(operands),
        out_specs=pl.BlockSpec(memory_space=pltpu.VMEM),
        scratch_shapes=[
            vmem((ROWS, 64), BF16),
            vmem((1, 4096), F32),
            vmem((128, 4096), BF16),
            vmem((64, 4096), BF16),
            vmem((TOKENS, 1024), BF16),
            vmem((TOKENS, 1024), BF16),
            vmem((SLOTS, 2, KEY_HEADS), F32),
            smem((1, SLOTS), I32),
            smem((1, SLOTS), I32),
            smem((1, 16), I32),
            smem((1, ROWS), I32),
            vmem((1, HEAD), F32),
            vmem((ROWS, TOKENS), F32),
            vmem((2, ROWS, HEAD), F32),
            vmem((ROWS, HEAD), BF16),
            vmem((PLANES, ROWS, HEAD), BF16),
            vmem((PLANES // 2, ROWS, HEAD), BF16),
            vmem((4, PLANES // 2, ROWS, HEAD), BF16),
            vmem((ROWS, HEAD), BF16),
            vmem((PLANES, ROWS, HEAD), BF16),
            vmem((4, PLANES, ROWS, HEAD), BF16),
            vmem((HEADS, ROWS, HEAD), F32),
            vmem((NEAR, 3, ROWS, HEAD), BF16),
            vmem((NEAR, 3, ROWS, HEAD), BF16),
            vmem((3, ROWS, HEAD), BF16),
            vmem((BLOCKS, 3, ROWS, HEAD), BF16),
            vmem((2 * ROWS, HEAD), BF16),
            vmem((NEAR, 2 * ROWS, HEAD), BF16),
            pltpu.SemaphoreType.DMA((12,)),
            pltpu.SemaphoreType.DMA((7,)),
            pltpu.SemaphoreType.DMA((7,)),
        ],
        compiler_params=pltpu.CompilerParams(
            collective_id=0, has_side_effects=True, vmem_limit_bytes=60 * 2**20
        ),
    )(*operands)
    return out[None]


def solution(mesh):
    in_specs = (
        P("section", None, "tp"),
        P("section", None),
        P("section", None, "tp"),
        P("section", None, "tp"),
        P("section", "tp", None, None),
        P("section", "tp", None, None),
        P("section", "tp", None, None),
        P("section", "tp"),
        P("section", "tp"),
        P("section", None),
        P("section", None),
    )
    out_specs = P("section", None, "tp")
    return jax.shard_map(local, mesh=mesh, in_specs=in_specs, out_specs=out_specs, check_vma=False)
```

time: 75.2 us -> 63.2 us (0.84)
  local copies, waits for them, and re-layouts: 8.59 us -> 1.28 us
  Pallas kernels: 66.2 us -> 61.8 us
    unnamed x25 -> x1, local copies, waits for them, and re-layouts: 8.59 us -> 1.28 us
    pallas_call x1, Pallas kernels: 66.2 us -> 61.8 us  [local(): pl.pallas_call(kernel, out_shape=jax.ShapeDtypeStruct((ROWS, 64), F32), i...]
where the time goes in v2:
time: 63.2 us; the launch traced here: 63.1 us
  Pallas kernels  61.8 us (98%)
  local copies, waits for them, and re-layouts  1.28 us (2%)
    pallas_call x1, Pallas kernels, local(): pl.pallas_call(kernel, out_shape=jax.ShapeDtypeStruct((ROWS, 64), F32), i...  61.8 us
    unnamed x1, local copies, waits for them, and re-layouts  1.28 us

profile of v2, /device:TPU:1, one launch (start us, length us, event | category | flops | bytes accessed | tf_op | source)
XLA Modules:
  0.0 63.1 jit_solution(10986476144838939757)
XLA Ops:
  0.0 61.8 %shard_map.118 = f32[8,64]{1,0:T(8,128)} custom-call(bf16[8,64]{1,0:T(8,128)(2,1)} %bitcast.17, f32[1,4096]{1,0:T(1,128)} %gain_hbm.1, bf16[96,4096]{1,0:T(8,128)(2,1)} %bitcast.13, bf16[64,4096]{1,0:T(8,128)(2,1)} %bitcast.14, bf16[512,1024]{1,0:T(8,128)(2,1)} %bitcast.11, bf16[512,1024]{1,0:T(8,128)(2,1)} %bitcast.12, f32[8,2,8]{2,1,0:T(2,128)} %bitcast.16, ...), custom_call_target="tpu_custom_call" | custom-call | tf_op jit(solution)/shard_map/pallas_call | solution.py:465
  61.8 1.3 %copy.17 = f32[1,8,64]{2,1,0:T(8,128)} copy(f32[1,8,64]{2,1,0:T(8,128)} %bitcast.15) | data formatting | bytes 4096

commit v3 on v2

--- a/solution.py
+++ b/solution.py
@@ -26,7 +26,9 @@
 MASKED = -1e30
 LOWEST = -1e25
 ROPE_BASE = 500000.0
+LINE_ORDER = (8, 7, 9, 6, 10, 5, 11, 4, 12, 3, 13, 2, 14, 1, 15)
 FARTHEST_FIRST = (7, 5, 3, 6, 1, 4, 2, 0)
+SHIFTED_FARTHEST_FIRST = (7, 6, 5, 4, 3, 2, 1, 0)
 TOGETHER = 2
 X_LINE, X_PLANE, Q_LINE, Q_PLANE, PART_NEAR, PART_FAR, OUT_NEAR = range(7)
 
@@ -134,14 +136,14 @@
     after = lax.rem(section + 1, sections)
     before = lax.rem(section + sections - 1, sections)
 
-    def near(d):
-        return lax.rem(mine + d, NEAR)
-
     def near_id(other):
         return {"tp": block * NEAR + other}
 
-    def far_id(where, other):
-        return {"section": where, "tp": other * NEAR + mine}
+    def far_id(other):
+        return {"tp": other * NEAR + mine}
+
+    def shifted_near_id(other):
+        return {"section": after, "tp": block * NEAR + other}
 
     def line_id(other):
         return {"tp": other * 4 + place}
@@ -154,33 +156,11 @@
     def greet(device):
         pl.semaphore_signal(barrier, inc=1, device_id=device, device_id_type=MESH)
 
-    def greet_line(k, carry):
+    for k in LINE_ORDER:
         greet(line_id(lax.rem(plane + k, PLANES)))
-        return carry
-
-    def greet_shift(k, carry):
-        for where in (before, after):
-            greet(plane_id(where, k))
-        return carry
-
-    def greet_far(k, carry):
-        other = lax.rem(block + k, BLOCKS)
-        for where in (before, after):
-            greet(far_id(where, other))
-        return carry
-
-    def greet_near(k, carry):
-        @pl.when(lax.rem(mine + k, 4) != place)
-        def _():
-            greet(near_id(near(k)))
-
-        return carry
-
-    lax.fori_loop(1, PLANES, greet_line, 0)
-    lax.fori_loop(0, 4, greet_shift, 0)
-    lax.fori_loop(1, BLOCKS, greet_far, 0)
-    lax.fori_loop(1, NEAR, greet_near, 0)
-    greetings = PLANES - 1 + 8 + 2 * (BLOCKS - 1) + NEAR - 4
+    for k in range(4):
+        greet(plane_id(before, k))
+    greetings = PLANES - 1 + 4
 
     moves = [
         pltpu.make_async_copy(src, dst, local_sem.at[k])
@@ -261,38 +241,26 @@
             device_id_type=MESH,
         ).start()
 
-    def start_far(stage, where, src, dst):
-        def go(d, carry):
-            other = lax.rem(block + BLOCKS // 2 + d, BLOCKS)
-            send(stage, src, dst.at[block], far_id(where, other))
-            return carry
-
-        lax.fori_loop(0, BLOCKS, go, 0)
+    def start_far(stage, src, dst):
+        for shift in (2, 1, 3):
+            send(stage, src, dst.at[block], far_id(lax.rem(block + shift, BLOCKS)))
+
+    chip, core = mine // 2, mine % 2
+    sibling = 2 * chip + 1 - core
 
     def start_near(stage, src, dst):
-        def go(d, carry):
-            send(stage, src, dst.at[mine], near_id(near(d)))
-            return carry
-
-        lax.fori_loop(1, NEAR, go, 0)
+        for k in FARTHEST_FIRST[:-1]:
+            for other in (0, 1):
+                send(stage, src, dst.at[mine], near_id(2 * (chip ^ k) + other))
+        send(stage, src, dst.at[mine], near_id(sibling))
 
     def start_line(stage, src, dst):
-        half = PLANES // 2
-        send(stage, src, dst.at[plane], line_id(lax.rem(plane + half, PLANES)))
-
-        def go(d, carry):
-            for shift in (half - d, half + d):
-                send(stage, src, dst.at[plane], line_id(lax.rem(plane + shift, PLANES)))
-            return carry
-
-        lax.fori_loop(1, half, go, 0)
+        for k in LINE_ORDER:
+            send(stage, src, dst.at[plane], line_id(lax.rem(plane + k, PLANES)))
 
     def start_plane(stage, where, src, dst):
-        def go(d, carry):
-            send(stage, src, dst.at[place], plane_id(where, lax.rem(place + 3 - d, 4)))
-            return carry
-
-        lax.fori_loop(0, 4, go, 0)
+        for k in (3, 2, 1, 0):
+            send(stage, src, dst.at[place], plane_id(where, place ^ k))
 
     def all_of(stage, part):
         return pltpu.make_async_remote_copy(
@@ -300,7 +268,7 @@
             dst_ref=part,
             send_sem=send_sem.at[stage],
             recv_sem=recv_sem.at[stage],
-            device_id=near_id(near(1)),
+            device_id=near_id(sibling),
             device_id_type=MESH,
         )
 
@@ -309,8 +277,8 @@
         X_PLANE: x_all,
         Q_LINE: q_line.at[pl.ds(0, PLANES - 1)],
         Q_PLANE: q_all,
-        PART_NEAR: part_all.at[pl.ds(0, NEAR - 1)],
-        PART_FAR: sum_all,
+        PART_NEAR: part_all,
+        PART_FAR: sum_all.at[pl.ds(0, BLOCKS - 1)],
         OUT_NEAR: att_all.at[pl.ds(0, NEAR - 1)],
     }
 
@@ -372,9 +340,8 @@
             heads[3 * z + k] = head
 
     hidden = jnp.concatenate([bias[...]] * 4, axis=0)
-    chip = mine // 2
-    for at in range(0, len(FARTHEST_FIRST), TOGETHER):
-        steps = FARTHEST_FIRST[at : at + TOGETHER]
+    for at in range(0, KEY_HEADS, TOGETHER):
+        steps = SHIFTED_FARTHEST_FIRST[at : at + TOGETHER]
         groups = [chip ^ k for k in steps]
         cols = [pl.ds(pl.multiple_of(g * HEAD, HEAD), HEAD) for g in groups]
         queries = [heads[pl.ds(4 * g, 4)].reshape(4 * ROWS, HEAD).astype(BF16) for g in groups]
@@ -382,43 +349,45 @@
         tops = [jnp.maximum(jnp.max(s, axis=1, keepdims=True), LOWEST) for s in scores]
         weights = [jnp.exp(s - t) for s, t in zip(scores, tops)]
         sums = [
-            jnp.dot(w.astype(BF16), values[:, c], preferred_element_type=F32).astype(BF16)
+            jnp.dot(w.astype(BF16), values[:, c], preferred_element_type=F32)
             for w, c in zip(weights, cols)
         ]
         totals = [jnp.sum(w, axis=1, keepdims=True) for w in weights]
+        if steps[-1] == 0:
+            new_key = jnp.concatenate([heads[QUERY_HEADS + chip]] * 4, axis=0)
+            new_value = jnp.concatenate([heads[QUERY_HEADS + KEY_HEADS + chip]] * 4, axis=0)
+            own = jnp.sum(queries[-1].astype(F32) * new_key, axis=1, keepdims=True) * SCALE
+            pair = lax.broadcasted_iota(I32, (4 * ROWS, 1), 0) // (2 * ROWS)
+            own = jnp.where((pair == core) & (block == 0), own, MASKED)
+            top = jnp.maximum(tops[-1], own)
+            old_weight, own_weight = jnp.exp(tops[-1] - top), jnp.exp(own - top)
+            totals[-1] = totals[-1] * old_weight + own_weight
+            sums[-1] = sums[-1] * old_weight + own_weight * new_value
+            tops[-1] = top
+        sums = [s.astype(BF16) for s in sums]
         for n, g in enumerate(groups):
             first, second = pack_stats(tops[n], totals[n], low, lane)
-            for core, stats in ((0, first), (1, second)):
-                part_send[2 * g + core, 0] = sums[n][16 * core : 16 * core + 8]
-                part_send[2 * g + core, 1] = sums[n][16 * core + 8 : 16 * core + 16]
-                part_send[2 * g + core, 2] = stats
-        for k, g in zip(steps, groups):
-            if k:
-                for other in (2 * g, 2 * g + 1):
-                    send(PART_NEAR, part_send.at[other], part_all.at[mine], near_id(other))
-    sibling = mine + 1 - 2 * (mine % 2)
-    send(PART_NEAR, part_send.at[sibling], part_all.at[mine], near_id(sibling))
-    part_all[mine] = part_send[mine]
-    own_query = jnp.concatenate([heads[2 * mine], heads[2 * mine + 1]], axis=0)
-    own_key = heads[QUERY_HEADS + mine // 2]
-    own_value = heads[QUERY_HEADS + KEY_HEADS + mine // 2]
-    own_score = (
-        jnp.sum(own_query * jnp.concatenate([own_key] * 2, axis=0), axis=1, keepdims=True) * SCALE
-    )
-    own_score = jnp.where(block == 0, own_score, MASKED)
+            for c, stats in ((0, first), (1, second)):
+                part_send[2 * g + c, 0] = sums[n][16 * c : 16 * c + 8]
+                part_send[2 * g + c, 1] = sums[n][16 * c + 8 : 16 * c + 16]
+                part_send[2 * g + c, 2] = stats
+        for g in groups:
+            for other in (2 * g, 2 * g + 1):
+                send(PART_NEAR, part_send.at[other], part_all.at[mine], shifted_near_id(other))
+
     arrived(PART_NEAR)
     stats = [unpack_stats(part_all[i, 2]) for i in range(NEAR)]
     top, total, weighted = merge(
-        [s[0] for s in stats] + [own_score],
-        [s[1] for s in stats] + [jnp.ones_like(own_score)],
-        [both(part_all[i]) for i in range(NEAR)]
-        + [jnp.concatenate([own_value] * 2, axis=0)],
+        [s[0] for s in stats],
+        [s[1] for s in stats],
+        [both(part_all[i]) for i in range(NEAR)],
     )
     sum_send[0] = weighted[:ROWS].astype(BF16)
     sum_send[1] = weighted[ROWS:].astype(BF16)
     sum_send[2] = pack_stats(top, total, low, lane)[0]
 
-    start_far(PART_FAR, after, sum_send, sum_all)
+    start_far(PART_FAR, sum_send, sum_all)
+    sum_all[block] = sum_send[...]
     arrived(PART_FAR)
     stats = [unpack_stats(sum_all[c, 2]) for c in range(BLOCKS)]
     top, total, weighted = merge(
@@ -461,10 +430,11 @@
         rows,
         freq,
     )
+    operands = [pltpu.with_memory_space_constraint(x, pltpu.HBM) for x in operands]
     vmem, smem = pltpu.VMEM, pltpu.SMEM
     out = pl.pallas_call(
         kernel,
-        out_shape=jax.ShapeDtypeStruct((ROWS, 64), F32),
+        out_shape=vmem((ROWS, 64), F32),
         in_specs=[pl.BlockSpec(memory_space=pltpu.HBM)] * len(operands),
         out_specs=pl.BlockSpec(memory_space=pltpu.VMEM),
         scratch_shapes=[
@@ -501,7 +471,7 @@
             pltpu.SemaphoreType.DMA((7,)),
         ],
         compiler_params=pltpu.CompilerParams(
-            collective_id=0, has_side_effects=True, vmem_limit_bytes=60 * 2**20
+            collective_id=0, has_side_effects=True, vmem_limit_bytes=40 * 2**20
         ),
     )(*operands)
     return out[None]

time: 63.2 us -> 60.7 us (0.960)
  Pallas kernels: 61.8 us -> 60 us
  local copies, waits for them, and re-layouts: 1.28 us -> 0.6 us
    pallas_call x1, Pallas kernels: 61.8 us -> 60 us  [local(): pl.pallas_call(kernel, out_shape=vmem((ROWS, 64), F32), in_specs=[pl.Bloc...]
    unnamed x1, local copies, waits for them, and re-layouts: 1.28 us -> 0.6 us
where the time goes in v3:
time: 60.7 us; the launch traced here: 60.6 us
  Pallas kernels  60 us (99%)
    pallas_call x1, Pallas kernels, local(): pl.pallas_call(kernel, out_shape=vmem((ROWS, 64), F32), in_specs=[pl.Bloc...  60 us

profile of v3, /device:TPU:1, one launch (start us, length us, event | category | flops | bytes accessed | tf_op | source)
XLA Modules:
  0.0 60.6 jit_solution(2105770400732257491)
XLA Ops:
  0.0 60.0 %shard_map.118 = f32[8,64]{1,0:T(8,128)S(1)} custom-call(bf16[8,64]{1,0:T(8,128)(2,1)} %bitcast.17, f32[1,4096]{1,0:T(1,128)} %gain_hbm.1, bf16[96,4096]{1,0:T(8,128)(2,1)} %bitcast.14, bf16[64,4096]{1,0:T(8,128)(2,1)} %bitcast.15, bf16[512,1024]{1,0:T(8,128)(2,1)} %bitcast.12, bf16[512,1024]{1,0:T(8,128)(2,1)} %bitcast.13, f32[8,2,8]{2,1,0:T(2,128)} %bitcast.16, ...), custom_call_target="tpu_custom_call" | custom-call | tf_op jit(solution)/shard_map/pallas_call | solution.py:435
  60.0 0.6 copy.17

commit v4 on v3

--- a/solution.py
+++ b/solution.py
@@ -59,27 +59,24 @@
     return tiles
 
 
-def unpack_stats(tile):
-    wide = tile.astype(F32)
-    part = [
-        jnp.concatenate([wide[:, at : at + 1], wide[:, at + 64 : at + 65]], axis=0)
-        for at in range(0, 48, 8)
-    ]
-    return part[0] + part[1] + part[2], part[3] + part[4] + part[5]
-
-
-def both(parts):
-    return jnp.concatenate([parts[0].astype(F32), parts[1].astype(F32)], axis=0)
-
-
-def merge(tops, totals, sums):
-    top = functools.reduce(jnp.maximum, tops)
-    total, weighted = 0.0, 0.0
-    for t, l, a in zip(tops, totals, sums):
-        factor = jnp.exp(t - top)
-        total = total + factor * l
-        weighted = weighted + factor * a
-    return top, total, weighted
+def merge(messages):
+    stats = []
+    for message in messages:
+        tile = message[2].astype(F32)
+        stats.append(tile + pltpu.roll(tile, HEAD - 8, 1) + pltpu.roll(tile, HEAD - 16, 1))
+    top = functools.reduce(jnp.maximum, stats)
+    total, sums = 0.0, [0.0, 0.0]
+    for message, stat in zip(messages, stats):
+        factor = jnp.exp(stat - top)
+        total = total + factor * pltpu.roll(stat, HEAD - 24, 1)
+        for h in range(2):
+            scale = jnp.broadcast_to(factor[:, 64 * h : 64 * h + 1], stat.shape)
+            sums[h] = sums[h] + scale * message[h].astype(F32)
+
+    def stacked(stat):
+        return jnp.concatenate([stat[:, 0:1], stat[:, 64:65]], axis=0)
+
+    return stacked(top), stacked(total), jnp.concatenate(sums, axis=0)
 
 
 def kernel(
@@ -116,6 +113,7 @@
     x_all,
     q_send,
     q_line,
+    q_pack,
     q_all,
     heads,
     part_send,
@@ -127,6 +125,7 @@
     local_sem,
     send_sem,
     recv_sem,
+    group_sem,
 ):
     section = lax.axis_index("section")
     tp = lax.axis_index("tp")
@@ -231,12 +230,12 @@
         moves[10].wait()
         moves[11].wait()
 
-    def send(stage, src, dst, device):
+    def send(stage, src, dst, device, sem=None):
         pltpu.make_async_remote_copy(
             src_ref=src,
             dst_ref=dst,
             send_sem=send_sem.at[stage],
-            recv_sem=recv_sem.at[stage],
+            recv_sem=recv_sem.at[stage] if sem is None else sem,
             device_id=device,
             device_id_type=MESH,
         ).start()
@@ -254,13 +253,31 @@
                 send(stage, src, dst.at[mine], near_id(2 * (chip ^ k) + other))
         send(stage, src, dst.at[mine], near_id(sibling))
 
+    def line_sem(stage, group):
+        return group_sem.at[0 if stage == X_LINE else 1, group]
+
     def start_line(stage, src, dst):
         for k in LINE_ORDER:
-            send(stage, src, dst.at[plane], line_id(lax.rem(plane + k, PLANES)))
+            other = line_id(lax.rem(plane + k, PLANES))
+            send(stage, src, dst.at[plane], other, line_sem(stage, block))
+
+    def groups_of_line(stage, buffer):
+        for shift in (0, 1, 3, 2):
+            group = lax.rem(block + shift, BLOCKS)
+            part = buffer.at[pl.ds(0, 4 if shift else 3)]
+            pltpu.make_async_remote_copy(
+                src_ref=part,
+                dst_ref=part,
+                send_sem=send_sem.at[stage],
+                recv_sem=line_sem(stage, group),
+                device_id=near_id(sibling),
+                device_id_type=MESH,
+            ).wait_recv()
+            yield group, [buffer[4 * group + k].astype(F32) for k in range(4)]
 
     def start_plane(stage, where, src, dst):
         for k in (3, 2, 1, 0):
-            send(stage, src, dst.at[place], plane_id(where, place ^ k))
+            send(stage, src, dst, plane_id(where, place ^ k))
 
     def all_of(stage, part):
         return pltpu.make_async_remote_copy(
@@ -292,19 +309,18 @@
     start_line(X_LINE, x_send, x_line)
     x_line[plane] = x_send[...]
     pl.when(jnp.logical_not(early))(prepare)
-    arrived(X_LINE)
-    for u in range(PLANES // 2):
-        tile = jnp.where(low, x_line[2 * u].astype(F32), x_line[2 * u + 1].astype(F32))
-        x_pack[u] = tile.astype(BF16)
-    start_plane(X_PLANE, after, x_pack, x_all)
+    for group, blocks in groups_of_line(X_LINE, x_line):
+        for u in range(2):
+            x_pack[group, u] = jnp.where(low, blocks[2 * u], blocks[2 * u + 1]).astype(BF16)
+        start_plane(X_PLANE, after, x_pack.at[group], x_all.at[place, group])
     arrived(X_PLANE)
 
     tiles = [None] * 32
     square = jnp.zeros((ROWS, HEAD), F32)
     for u in range(PLANES // 2):
         for j in range(2):
-            even = x_all[2 * j, u].astype(F32)
-            odd = x_all[2 * j + 1, u].astype(F32)
+            even = x_all[2 * j, u // 2, u % 2].astype(F32)
+            odd = x_all[2 * j + 1, u // 2, u % 2].astype(F32)
             square = square + even * even + odd * odd
             tiles[4 * u + j] = jnp.where(low, even, pltpu.roll(odd, 64, 1))
             tiles[4 * u + 2 + j] = jnp.where(low, pltpu.roll(even, 64, 1), odd)
@@ -325,19 +341,32 @@
 
     start_line(Q_LINE, q_send, q_line)
     q_line[plane] = q_send[...]
-    arrived(Q_LINE)
-    start_plane(Q_PLANE, before, q_line, q_all)
+    quarter = lane // 32
+    for group, blocks in groups_of_line(Q_LINE, q_line):
+        for k in range(3):
+            moved = pltpu.roll(blocks[3], 96 - 32 * k, 1)
+            q_pack[group, k] = jnp.where(quarter == 3 - place, moved, blocks[k]).astype(BF16)
+        start_plane(Q_PLANE, before, q_pack.at[group], q_all.at[place, group])
     arrived(Q_PLANE)
 
     cosine, sine = turn[0], turn[1]
-    for z in range(PLANES):
-        b = [q_all[p, z].astype(F32) for p in range(4)]
-        for k, edge in enumerate((96, 64, 32)):
-            head = jnp.where(lane < edge, b[k], b[k + 1])
-            if 3 * z + k < QUERY_HEADS + KEY_HEADS:
-                head = head * cosine + pltpu.roll(head, 64, 1) * sine
-                head = head.astype(BF16).astype(F32)
-            heads[3 * z + k] = head
+    for c in range(BLOCKS):
+        blocks = []
+        for p in range(4):
+            held = [q_all[p, c, k].astype(F32) for k in range(3)]
+            fourth = pltpu.roll(held[0], 32, 1)
+            for k in (1, 2):
+                moved = pltpu.roll(held[k], 32 * (k + 1), 1)
+                fourth = jnp.where(quarter == (4 - p + k) % 4, moved, fourth)
+            blocks.append(held + [fourth])
+        for z in range(4):
+            for k, edge in enumerate((96, 64, 32)):
+                h = 3 * (4 * c + z) + k
+                head = jnp.where(lane < edge, blocks[k][z], blocks[k + 1][z])
+                if h < QUERY_HEADS + KEY_HEADS:
+                    head = head * cosine + pltpu.roll(head, 64, 1) * sine
+                    head = head.astype(BF16).astype(F32)
+                heads[h] = head
 
     hidden = jnp.concatenate([bias[...]] * 4, axis=0)
     for at in range(0, KEY_HEADS, TOGETHER):
@@ -376,12 +405,7 @@
                 send(PART_NEAR, part_send.at[other], part_all.at[mine], shifted_near_id(other))
 
     arrived(PART_NEAR)
-    stats = [unpack_stats(part_all[i, 2]) for i in range(NEAR)]
-    top, total, weighted = merge(
-        [s[0] for s in stats],
-        [s[1] for s in stats],
-        [both(part_all[i]) for i in range(NEAR)],
-    )
+    top, total, weighted = merge([part_all[i] for i in range(NEAR)])
     sum_send[0] = weighted[:ROWS].astype(BF16)
     sum_send[1] = weighted[ROWS:].astype(BF16)
     sum_send[2] = pack_stats(top, total, low, lane)[0]
@@ -389,12 +413,7 @@
     start_far(PART_FAR, sum_send, sum_all)
     sum_all[block] = sum_send[...]
     arrived(PART_FAR)
-    stats = [unpack_stats(sum_all[c, 2]) for c in range(BLOCKS)]
-    top, total, weighted = merge(
-        [s[0] for s in stats],
-        [s[1] for s in stats],
-        [both(sum_all[c]) for c in range(BLOCKS)],
-    )
+    top, total, weighted = merge([sum_all[c] for c in range(BLOCKS)])
     att_send[...] = (weighted / total).astype(BF16)
     att_all[mine] = att_send[...]
     start_near(OUT_NEAR, att_send, att_all)
@@ -404,7 +423,7 @@
         pair = att_all[i].astype(F32)
         pieces += [pair[:ROWS], pair[ROWS:]]
     attended = jnp.concatenate(pieces, axis=1).astype(BF16)
-    x_here = x_all[place, plane // 2].astype(F32)
+    x_here = x_all[place, block, plane % 4 // 2].astype(F32)
     x_here = jnp.where(plane % 2 == 0, x_here, pltpu.roll(x_here, 64, 1))[:, :64]
     out_ref[...] = nt(attended, wo[...]) + x_here
 
@@ -454,11 +473,12 @@
             vmem((2, ROWS, HEAD), F32),
             vmem((ROWS, HEAD), BF16),
             vmem((PLANES, ROWS, HEAD), BF16),
-            vmem((PLANES // 2, ROWS, HEAD), BF16),
-            vmem((4, PLANES // 2, ROWS, HEAD), BF16),
+            vmem((BLOCKS, 2, ROWS, HEAD), BF16),
+            vmem((4, BLOCKS, 2, ROWS, HEAD), BF16),
             vmem((ROWS, HEAD), BF16),
             vmem((PLANES, ROWS, HEAD), BF16),
-            vmem((4, PLANES, ROWS, HEAD), BF16),
+            vmem((BLOCKS, 3, ROWS, HEAD), BF16),
+            vmem((4, BLOCKS, 3, ROWS, HEAD), BF16),
             vmem((HEADS, ROWS, HEAD), F32),
             vmem((NEAR, 3, ROWS, HEAD), BF16),
             vmem((NEAR, 3, ROWS, HEAD), BF16),
@@ -469,6 +489,7 @@
             pltpu.SemaphoreType.DMA((12,)),
             pltpu.SemaphoreType.DMA((7,)),
             pltpu.SemaphoreType.DMA((7,)),
+            pltpu.SemaphoreType.DMA((2, BLOCKS)),
         ],
         compiler_params=pltpu.CompilerParams(
             collective_id=0, has_side_effects=True, vmem_limit_bytes=40 * 2**20

time: 60.7 us -> 60.1 us (level)
    pallas_call x1, Pallas kernels: 60 us -> 59.4 us  [local(): pl.pallas_call(kernel, out_shape=vmem((ROWS, 64), F32), in_specs=[pl.Bloc...]
where the time goes in v4:
time: 60.1 us; the launch traced here: 60 us
  Pallas kernels  59.4 us (99%)
    pallas_call x1, Pallas kernels, local(): pl.pallas_call(kernel, out_shape=vmem((ROWS, 64), F32), in_specs=[pl.Bloc...  59.4 us

profile of v4, /device:TPU:1, one launch (start us, length us, event | category | flops | bytes accessed | tf_op | source)
XLA Modules:
  0.0 60.0 jit_solution(14545600263610584428)
XLA Ops:
  0.0 59.4 %shard_map.118 = f32[8,64]{1,0:T(8,128)S(1)} custom-call(bf16[8,64]{1,0:T(8,128)(2,1)} %bitcast.17, f32[1,4096]{1,0:T(1,128)} %gain_hbm.1, bf16[96,4096]{1,0:T(8,128)(2,1)} %bitcast.14, bf16[64,4096]{1,0:T(8,128)(2,1)} %bitcast.15, bf16[512,1024]{1,0:T(8,128)(2,1)} %bitcast.12, bf16[512,1024]{1,0:T(8,128)(2,1)} %bitcast.13, f32[8,2,8]{2,1,0:T(2,128)} %bitcast.16, ...), custom_call_target="tpu_custom_call" | custom-call | tf_op jit(solution)/shard_map/pallas_call | solution.py:454
  59.4 0.6 copy.17

commit v5 on v4

--- a/solution.py
+++ b/solution.py
@@ -30,7 +30,8 @@
 FARTHEST_FIRST = (7, 5, 3, 6, 1, 4, 2, 0)
 SHIFTED_FARTHEST_FIRST = (7, 6, 5, 4, 3, 2, 1, 0)
 TOGETHER = 2
-X_LINE, X_PLANE, Q_LINE, Q_PLANE, PART_NEAR, PART_FAR, OUT_NEAR = range(7)
+X_LINE, X_PLANE, Q_LINE, Q_PLANE, PART_NEAR, PART_FAR, OUT_NEAR, PART_LEAD = range(8)
+LEAD_SECTION, LEAD = 0, 1
 
 
 def nt(left, right):
@@ -122,6 +123,7 @@
     sum_all,
     att_send,
     att_all,
+    lead_all,
     local_sem,
     send_sem,
     recv_sem,
@@ -247,11 +249,23 @@
     chip, core = mine // 2, mine % 2
     sibling = 2 * chip + 1 - core
 
+    lead_group = (section == LEAD_SECTION) & (block == LEAD // NEAR)
+    is_lead = lead_group & (mine == LEAD % NEAR)
+
     def start_near(stage, src, dst):
-        for k in FARTHEST_FIRST[:-1]:
-            for other in (0, 1):
-                send(stage, src, dst.at[mine], near_id(2 * (chip ^ k) + other))
-        send(stage, src, dst.at[mine], near_id(sibling))
+        for k in FARTHEST_FIRST:
+            for c in (0, 1):
+                other = 2 * (chip ^ k) + c
+                skipped = lead_group & (other == LEAD % NEAR) if c == LEAD % 2 else None
+                if k == 0:
+                    skipped = core == c if skipped is None else skipped | (core == c)
+                if skipped is None:
+                    send(stage, src, dst.at[mine], near_id(other))
+                else:
+
+                    @pl.when(jnp.logical_not(skipped))
+                    def _():
+                        send(stage, src, dst.at[mine], near_id(other))
 
     def line_sem(stage, group):
         return group_sem.at[0 if stage == X_LINE else 1, group]
@@ -411,13 +425,31 @@
     sum_send[2] = pack_stats(top, total, low, lane)[0]
 
     start_far(PART_FAR, sum_send, sum_all)
+    to_lead = (section == LEAD_SECTION) & (tp != LEAD)
+
+    @pl.when(to_lead)
+    def _():
+        send(PART_LEAD, sum_send, lead_all.at[tp], {"tp": LEAD})
+
     sum_all[block] = sum_send[...]
     arrived(PART_FAR)
     top, total, weighted = merge([sum_all[c] for c in range(BLOCKS)])
     att_send[...] = (weighted / total).astype(BF16)
     att_all[mine] = att_send[...]
     start_near(OUT_NEAR, att_send, att_all)
-    arrived(OUT_NEAR)
+
+    @pl.when(jnp.logical_not(is_lead))
+    def _():
+        arrived(OUT_NEAR)
+
+    @pl.when(is_lead)
+    def _():
+        lead_all[LEAD] = sum_send[...]
+        all_of(PART_LEAD, lead_all.at[pl.ds(0, BLOCKS * NEAR - 1)]).wait_recv()
+        for i in range(NEAR):
+            _, total, weighted = merge([lead_all[NEAR * c + i] for c in range(BLOCKS)])
+            att_all[i] = (weighted / total).astype(BF16)
+
     pieces = []
     for i in range(NEAR):
         pair = att_all[i].astype(F32)
@@ -428,7 +460,21 @@
     out_ref[...] = nt(attended, wo[...]) + x_here
 
     for stage, part in expected.items():
-        all_of(stage, part).wait_send()
+        if stage != OUT_NEAR:
+            all_of(stage, part).wait_send()
+    fewer = lead_group & jnp.logical_not(is_lead)
+
+    @pl.when(fewer)
+    def _():
+        all_of(OUT_NEAR, att_all.at[pl.ds(0, NEAR - 2)]).wait_send()
+
+    @pl.when(jnp.logical_not(fewer))
+    def _():
+        all_of(OUT_NEAR, att_all.at[pl.ds(0, NEAR - 1)]).wait_send()
+
+    @pl.when(to_lead)
+    def _():
+        all_of(PART_LEAD, sum_send).wait_send()
 
 
 def local(x, gain, wq, wo, key_codes, value_codes, scale_table, owner, number, lengths, rows):
@@ -486,9 +532,10 @@
             vmem((BLOCKS, 3, ROWS, HEAD), BF16),
             vmem((2 * ROWS, HEAD), BF16),
             vmem((NEAR, 2 * ROWS, HEAD), BF16),
+            vmem((BLOCKS * NEAR, 3, ROWS, HEAD), BF16),
             pltpu.SemaphoreType.DMA((12,)),
-            pltpu.SemaphoreType.DMA((7,)),
-            pltpu.SemaphoreType.DMA((7,)),
+            pltpu.SemaphoreType.DMA((8,)),
+            pltpu.SemaphoreType.DMA((8,)),
             pltpu.SemaphoreType.DMA((2, BLOCKS)),
         ],
         compiler_params=pltpu.CompilerParams(

time: 60.1 us -> 58.2 us (0.968)
  Pallas kernels: 59.4 us -> 57.4 us
    pallas_call x1, Pallas kernels: 59.4 us -> 57.4 us  [local(): pl.pallas_call(kernel, out_shape=vmem((ROWS, 64), F32), in_specs=[pl.Bloc...]
where the time goes in v5:
time: 58.2 us; the launch traced here: 58 us
  Pallas kernels  57.4 us (99%)
  local copies, waits for them, and re-layouts  0.6 us (1%)
    pallas_call x1, Pallas kernels, local(): pl.pallas_call(kernel, out_shape=vmem((ROWS, 64), F32), in_specs=[pl.Bloc...  57.4 us

profile of v5, /device:TPU:1, one launch (start us, length us, event | category | flops | bytes accessed | tf_op | source)
XLA Modules:
  0.0 58.0 jit_solution(17762547297335658290)
XLA Ops:
  0.0 57.4 %shard_map.118 = f32[8,64]{1,0:T(8,128)S(1)} custom-call(bf16[8,64]{1,0:T(8,128)(2,1)} %bitcast.17, f32[1,4096]{1,0:T(1,128)} %gain_hbm.1, bf16[96,4096]{1,0:T(8,128)(2,1)} %bitcast.14, bf16[64,4096]{1,0:T(8,128)(2,1)} %bitcast.15, bf16[512,1024]{1,0:T(8,128)(2,1)} %bitcast.12, bf16[512,1024]{1,0:T(8,128)(2,1)} %bitcast.13, f32[8,2,8]{2,1,0:T(2,128)} %bitcast.16, ...), custom_call_target="tpu_custom_call" | custom-call | tf_op jit(solution)/shard_map/pallas_call | solution.py:500
  57.4 0.6 %copy.17 = f32[1,8,64]{2,1,0:T(8,128)} copy(f32[1,8,64]{2,1,0:T(8,128)S(1)} %bitcast.11) | data formatting | bytes 4096

commit v6 on v5

--- a/solution.py
+++ b/solution.py
@@ -28,8 +28,6 @@
 ROPE_BASE = 500000.0
 LINE_ORDER = (8, 7, 9, 6, 10, 5, 11, 4, 12, 3, 13, 2, 14, 1, 15)
 FARTHEST_FIRST = (7, 5, 3, 6, 1, 4, 2, 0)
-SHIFTED_FARTHEST_FIRST = (7, 6, 5, 4, 3, 2, 1, 0)
-TOGETHER = 2
 X_LINE, X_PLANE, Q_LINE, Q_PLANE, PART_NEAR, PART_FAR, OUT_NEAR, PART_LEAD = range(8)
 LEAD_SECTION, LEAD = 0, 1
 
@@ -382,41 +380,46 @@
                     head = head.astype(BF16).astype(F32)
                 heads[h] = head
 
-    hidden = jnp.concatenate([bias[...]] * 4, axis=0)
-    for at in range(0, KEY_HEADS, TOGETHER):
-        steps = SHIFTED_FARTHEST_FIRST[at : at + TOGETHER]
-        groups = [chip ^ k for k in steps]
-        cols = [pl.ds(pl.multiple_of(g * HEAD, HEAD), HEAD) for g in groups]
-        queries = [heads[pl.ds(4 * g, 4)].reshape(4 * ROWS, HEAD).astype(BF16) for g in groups]
-        scores = [nt(q, keys[:, c]) * SCALE + hidden for q, c in zip(queries, cols)]
-        tops = [jnp.maximum(jnp.max(s, axis=1, keepdims=True), LOWEST) for s in scores]
-        weights = [jnp.exp(s - t) for s, t in zip(scores, tops)]
-        sums = [
-            jnp.dot(w.astype(BF16), values[:, c], preferred_element_type=F32)
-            for w, c in zip(weights, cols)
-        ]
-        totals = [jnp.sum(w, axis=1, keepdims=True) for w in weights]
-        if steps[-1] == 0:
-            new_key = jnp.concatenate([heads[QUERY_HEADS + chip]] * 4, axis=0)
-            new_value = jnp.concatenate([heads[QUERY_HEADS + KEY_HEADS + chip]] * 4, axis=0)
-            own = jnp.sum(queries[-1].astype(F32) * new_key, axis=1, keepdims=True) * SCALE
-            pair = lax.broadcasted_iota(I32, (4 * ROWS, 1), 0) // (2 * ROWS)
-            own = jnp.where((pair == core) & (block == 0), own, MASKED)
-            top = jnp.maximum(tops[-1], own)
-            old_weight, own_weight = jnp.exp(tops[-1] - top), jnp.exp(own - top)
-            totals[-1] = totals[-1] * old_weight + own_weight
-            sums[-1] = sums[-1] * old_weight + own_weight * new_value
-            tops[-1] = top
-        sums = [s.astype(BF16) for s in sums]
-        for n, g in enumerate(groups):
-            first, second = pack_stats(tops[n], totals[n], low, lane)
-            for c, stats in ((0, first), (1, second)):
-                part_send[2 * g + c, 0] = sums[n][16 * c : 16 * c + 8]
-                part_send[2 * g + c, 1] = sums[n][16 * c + 8 : 16 * c + 16]
-                part_send[2 * g + c, 2] = stats
-        for g in groups:
-            for other in (2 * g, 2 * g + 1):
-                send(PART_NEAR, part_send.at[other], part_all.at[mine], shifted_near_id(other))
+    hidden = jnp.concatenate([bias[...]] * 8, axis=0)
+    blank = jnp.zeros((4 * ROWS, HEAD), F32)
+    for step in (3, 2, 1, 0):
+        pair = (chip // 2) ^ step
+        cols = pl.ds(pl.multiple_of(pair * 2 * HEAD, 2 * HEAD), 2 * HEAD)
+        rows = heads[pl.ds(8 * pair, 8)].reshape(8 * ROWS, HEAD)
+        query = jnp.concatenate(
+            [
+                jnp.concatenate([rows[: 4 * ROWS], blank], axis=1),
+                jnp.concatenate([blank, rows[4 * ROWS :]], axis=1),
+            ],
+            axis=0,
+        ).astype(BF16)
+        score = nt(query, keys[:, cols]) * SCALE + hidden
+        top = jnp.maximum(jnp.max(score, axis=1, keepdims=True), LOWEST)
+        weight = jnp.exp(score - top)
+        both = jnp.dot(weight.astype(BF16), values[:, cols], preferred_element_type=F32)
+        weighted = jnp.concatenate([both[: 4 * ROWS, :HEAD], both[4 * ROWS :, HEAD:]], axis=0)
+        total = jnp.sum(weight, axis=1, keepdims=True)
+        if step == 0:
+            key = QUERY_HEADS + 2 * pair
+            new_key = jnp.concatenate([heads[key]] * 4 + [heads[key + 1]] * 4, axis=0)
+            key = key + KEY_HEADS
+            new_value = jnp.concatenate([heads[key]] * 4 + [heads[key + 1]] * 4, axis=0)
+            own = jnp.sum(rows * new_key, axis=1, keepdims=True) * SCALE
+            place_of = lax.broadcasted_iota(I32, (8 * ROWS, 1), 0) // (2 * ROWS)
+            own = jnp.where((place_of == mine % 4) & (block == 0), own, MASKED)
+            peak = jnp.maximum(top, own)
+            old_weight, own_weight = jnp.exp(top - peak), jnp.exp(own - peak)
+            total = total * old_weight + own_weight
+            weighted = weighted * old_weight + own_weight * new_value
+            top = peak
+        weighted = weighted.astype(BF16)
+        for n, stats in enumerate(pack_stats(top, total, low, lane)):
+            part_send[4 * pair + n, 0] = weighted[16 * n : 16 * n + 8]
+            part_send[4 * pair + n, 1] = weighted[16 * n + 8 : 16 * n + 16]
+            part_send[4 * pair + n, 2] = stats
+        for n in range(4):
+            other = 4 * pair + n
+            send(PART_NEAR, part_send.at[other], part_all.at[mine], shifted_near_id(other))
 
     arrived(PART_NEAR)
     top, total, weighted = merge([part_all[i] for i in range(NEAR)])

time: 58.2 us -> 58.2 us (level)
  no operation moved by 1% of the time
where the time goes in v6:
time: 58.2 us; the launch traced here: 58.1 us
  Pallas kernels  57.5 us (99%)
  local copies, waits for them, and re-layouts  0.6 us (1%)
    pallas_call x1, Pallas kernels, local(): pl.pallas_call(kernel, out_shape=vmem((ROWS, 64), F32), in_specs=[pl.Bloc...  57.5 us

profile of v6, /device:TPU:1, one launch (start us, length us, event | category | flops | bytes accessed | tf_op | source)
XLA Modules:
  0.0 58.1 jit_solution(10615509682256596652)
XLA Ops:
  0.0 57.5 %shard_map.118 = f32[8,64]{1,0:T(8,128)S(1)} custom-call(bf16[8,64]{1,0:T(8,128)(2,1)} %bitcast.17, f32[1,4096]{1,0:T(1,128)} %gain_hbm.1, bf16[96,4096]{1,0:T(8,128)(2,1)} %bitcast.14, bf16[64,4096]{1,0:T(8,128)(2,1)} %bitcast.15, bf16[512,1024]{1,0:T(8,128)(2,1)} %bitcast.12, bf16[512,1024]{1,0:T(8,128)(2,1)} %bitcast.13, f32[8,2,8]{2,1,0:T(2,128)} %bitcast.16, ...), custom_call_target="tpu_custom_call" | custom-call | tf_op jit(solution)/shard_map/pallas_call | solution.py:503
  57.5 0.6 %copy.17 = f32[1,8,64]{2,1,0:T(8,128)} copy(f32[1,8,64]{2,1,0:T(8,128)S(1)} %bitcast.11) | data formatting | bytes 4096

commit v7 on v6

--- a/solution.py
+++ b/solution.py
@@ -241,8 +241,11 @@
         ).start()
 
     def start_far(stage, src, dst):
-        for shift in (2, 1, 3):
-            send(stage, src, dst.at[block], far_id(lax.rem(block + shift, BLOCKS)))
+        for other in range(BLOCKS):
+
+            @pl.when(block != other)
+            def _():
+                send(stage, src, dst.at[block], far_id(other))
 
     chip, core = mine // 2, mine % 2
     sibling = 2 * chip + 1 - core

time: 58.2 us -> 58.2 us (level)
  no operation moved by 1% of the time
where the time goes in v7:
time: 58.2 us; the launch traced here: 58.1 us
  Pallas kernels  57.5 us (99%)
  local copies, waits for them, and re-layouts  0.6 us (1%)
    pallas_call x1, Pallas kernels, local(): pl.pallas_call(kernel, out_shape=vmem((ROWS, 64), F32), in_specs=[pl.Bloc...  57.5 us

profile of v7, /device:TPU:1, one launch (start us, length us, event | category | flops | bytes accessed | tf_op | source)
XLA Modules:
  0.0 58.1 jit_solution(1288847665426208508)
XLA Ops:
  0.0 57.5 %shard_map.118 = f32[8,64]{1,0:T(8,128)S(1)} custom-call(bf16[8,64]{1,0:T(8,128)(2,1)} %bitcast.17, f32[1,4096]{1,0:T(1,128)} %gain_hbm.1, bf16[96,4096]{1,0:T(8,128)(2,1)} %bitcast.14, bf16[64,4096]{1,0:T(8,128)(2,1)} %bitcast.15, bf16[512,1024]{1,0:T(8,128)(2,1)} %bitcast.12, bf16[512,1024]{1,0:T(8,128)(2,1)} %bitcast.13, f32[8,2,8]{2,1,0:T(2,128)} %bitcast.16, ...), custom_call_target="tpu_custom_call" | custom-call | tf_op jit(solution)/shard_map/pallas_call | solution.py:506
  57.5 0.6 %copy.17 = f32[1,8,64]{2,1,0:T(8,128)} copy(f32[1,8,64]{2,1,0:T(8,128)S(1)} %bitcast.11) | data formatting | bytes 4096
